TPU v7x, 32 devices: a whole 2x2x4 slice. The times are simulated.
32 devices in a mesh: groups: 2 (over x), expert: 16 (over z, y, core).
Axes of the slice: x: 2, y: 2, z: 4, core: 2. Of those that a mesh axis runs over, the one named last changes fastest.
Arguments:
- hidden_in: bfloat16 [4096, 2048], P(('groups', 'expert')), parts along dimension 0, may hold values from -6 to 6
- norm_gain: float32 [2048], replicated, may hold values from 0.1 to 1.9
- router_weight: bfloat16 [2048, 16], replicated, may hold values from -0.125 to 0.125
- expert_ids: int32 [4096, 8], P(('groups', 'expert')), parts along dimension 0, may hold values from 0 to 15, all different within a row; in each aligned block of 128 rows (0 to 127, 128 to 255, ...) at most 96 rows name the same one
- w_gate: bfloat16 [16, 2048, 768], P('expert'), may hold values from -0.125 to 0.125
- w_up: bfloat16 [16, 2048, 768], P('expert'), may hold values from -0.125 to 0.125
- w_down: bfloat16 [16, 768, 2048], P('expert'), may hold values from -0.21875 to 0.21875
Outputs:
- combined: bfloat16 [4096, 2048], P(('groups', 'expert')), parts along dimension 0
There are 2 independent parts, one for each index of `groups`. A program takes and returns all parts, laid end to end along the dimension named above; an argument that names none is the same for every part. Nothing has to cross between parts.
Inputs may be any that keep to these rules, and one draw needn't show every extreme that they name: `expert_ids`: each row names 8 different experts; within each aligned block of 128 rows (the rows of one device) no expert is named by more than 96 rows, a bound that some block reaches.
All inputs are finite; a program needn't handle non-finite values.
Results may differ from a plain program's by a relative error of at most 0.0074.
Values may be sent and summed in bfloat16 or wider, within the bound.
No kernel may reach another device: no remote copies, remote signals or barrier semaphores. Data moves between devices by JAX's collectives and lax.ppermute only.
A program may use at most 128 MiB of HBM per device.

v0:
```python
import functools

import jax
import jax.numpy as jnp
from jax import lax
from jax.experimental import pallas as pl
from jax.experimental.pallas import tpu as pltpu
from jax.sharding import PartitionSpec as P

MIB = 1 << 20


def pack_kernel(*refs):
    sources, outs, held, sems = refs[:4], refs[4:-5], refs[-5:-1], refs[-1]
    copies = [
        pltpu.make_async_copy(source, place, sems.at[i])
        for i, (source, place) in enumerate(zip(sources, held))
    ]
    for copy in copies:
        copy.start()
    for copy in copies:
        copy.wait()
    x_ref, gain_ref, router_ref, ids_ref = held
    rows, width = x_ref.shape
    num_experts = router_ref.shape[0]
    as_float = x_ref[...].astype(jnp.float32)
    inv_rms = lax.rsqrt(jnp.mean(as_float * as_float, axis=1, keepdims=True) + 1e-06)
    normed = (as_float * inv_rms * gain_ref[...]).astype(jnp.bfloat16)
    half = rows // 2
    ranges = [(0, rows), (0, half), (half, rows)]
    for (low, high), out_ref in zip(ranges, outs):
        out_ref[:, :width] = normed[low:high]
    logits = lax.dot_general(
        router_ref[...], normed, (((1,), (1,)), ((), ())), preferred_element_type=jnp.float32
    )
    ids = ids_ref[...]
    expert = lax.broadcasted_iota(jnp.int32, (num_experts, rows), 0)
    named = expert == ids[0:1, :]
    for k in range(1, ids.shape[0]):
        named = named | (expert == ids[k : k + 1, :])
    picked = jnp.where(named, jnp.exp(logits), 0.0)
    weight = picked / jnp.sum(picked, axis=0, keepdims=True)
    high = weight.astype(jnp.bfloat16).astype(jnp.float32)
    parts = [high, weight - high]
    spare = outs[0].shape[1] - width - 2 * num_experts
    if spare:
        parts.append(jnp.zeros((spare, rows), jnp.float32))
    beside = jnp.concatenate(parts, axis=0).T.astype(jnp.bfloat16)
    for (low, high), out_ref in zip(ranges, outs):
        out_ref[:, width:] = beside[low:high]


def pack(hidden_in, norm_gain, router_weight, expert_ids):
    rows, width = hidden_in.shape
    lanes = -(-2 * router_weight.shape[1] // 128) * 128
    sources = [hidden_in, norm_gain[None, :], router_weight.T, expert_ids.T]
    return pl.pallas_call(
        pack_kernel,
        out_shape=[
            jax.ShapeDtypeStruct((r, width + lanes), jnp.bfloat16)
            for r in (rows, rows // 2, rows // 2)
        ],
        in_specs=[pl.BlockSpec(memory_space=pl.ANY)] * len(sources),
        scratch_shapes=[pltpu.VMEM(a.shape, a.dtype) for a in sources]
        + [pltpu.SemaphoreType.DMA((len(sources),))],
        compiler_params=pltpu.CompilerParams(vmem_limit_bytes=58 * MIB),
        name="pack_rows",
    )(*sources)


def ffn_kernel(heights, splits, *refs):
    count = len(heights)
    shards = refs[:count]
    gate_ref, up_ref, down_ref, mine_ref = refs[count : count + 4]
    outs = refs[count + 4 : count + 4 + len(splits)]
    x_ref, hidden_ref, weight_ref = refs[-3:]
    width, depth = gate_ref.shape
    top = 0
    for shard, height in zip(shards, heights):
        x_ref[top : top + height, :] = shard[:, :width]
        parts = shard[:, width:].astype(jnp.float32) * mine_ref[...]
        weight_ref[top : top + height, :] = jnp.sum(parts, axis=1, keepdims=True)
        top += height
    tile = 256 if depth % 256 == 0 else depth

    @pl.loop(0, depth // tile)
    def _(j):
        at = pl.ds(pl.multiple_of(j * tile, tile), tile)
        gate_act = jnp.dot(x_ref[...], gate_ref[:, at], preferred_element_type=jnp.float32)
        up_act = jnp.dot(x_ref[...], up_ref[:, at], preferred_element_type=jnp.float32)
        hidden = gate_act / (1.0 + jnp.exp(-gate_act)) * up_act
        hidden_ref[:, at] = hidden.astype(jnp.bfloat16)

    step = 512 if width % 512 == 0 else width

    @pl.loop(0, width // step)
    def _(j):
        at = pl.ds(pl.multiple_of(j * step, step), step)
        out = jnp.dot(hidden_ref[...], down_ref[:, at], preferred_element_type=jnp.float32)
        done = (out * weight_ref[...]).astype(jnp.bfloat16)
        first = 0
        for out_ref, height in zip(outs, splits):
            out_ref[:, at] = done[first : first + height]
            first += height


def ffn(shards, splits, w_gate, w_up, w_down, mine):
    width, depth = w_gate.shape
    heights = [s.shape[0] for s in shards]
    rows = sum(heights)
    return pl.pallas_call(
        functools.partial(ffn_kernel, heights, splits),
        out_shape=[jax.ShapeDtypeStruct((h, width), jnp.bfloat16) for h in splits],
        scratch_shapes=[
            pltpu.VMEM((rows, width), jnp.bfloat16),
            pltpu.VMEM((rows, depth), jnp.bfloat16),
            pltpu.VMEM((rows, 1), jnp.float32),
        ],
        compiler_params=pltpu.CompilerParams(vmem_limit_bytes=20 * MIB),
        cost_estimate=pl.CostEstimate(
            flops=6 * rows * width * depth,
            bytes_accessed=rows * width,
            transcendentals=0,
        ),
        name="expert_ffn",
    )(*shards, w_gate, w_up, w_down, mine)


def beside_kernel(x_ref, *refs):
    refs[-1][...] = x_ref[...]


def beside_weights(x, *weights):
    return pl.pallas_call(
        beside_kernel,
        out_shape=jax.ShapeDtypeStruct(x.shape, x.dtype),
        in_specs=[pl.BlockSpec(memory_space=pltpu.VMEM)] * (1 + len(weights)),
        out_specs=pl.BlockSpec(memory_space=pltpu.VMEM),
        compiler_params=pltpu.CompilerParams(vmem_limit_bytes=16 * MIB),
        name="beside_weights",
    )(x, *weights)


def join_kernel(*refs):
    out_ref, top = refs[-1], 0
    for ref in refs[:-1]:
        out_ref[top : top + ref.shape[0], :] = ref[...]
        top += ref.shape[0]


def join(arrays):
    rows = sum(a.shape[0] for a in arrays)
    return pl.pallas_call(
        join_kernel,
        out_shape=jax.ShapeDtypeStruct((rows, arrays[0].shape[1]), arrays[0].dtype),
        compiler_params=pltpu.CompilerParams(vmem_limit_bytes=16 * MIB),
        name="join_rows",
    )(*arrays)


def combine_kernel(parts, *refs):
    out_ref, at, top = refs[-1], 0, 0
    for height, offsets in parts:
        total = 0.0
        for offset in offsets:
            total = total + refs[at][offset : offset + height, :].astype(jnp.float32)
            at += 1
        out_ref[top : top + height, :] = total.astype(out_ref.dtype)
        top += height


def combine(*parts):
    arrays = [array for _, terms in parts for array, _ in terms]
    heights = [(height, [offset for _, offset in terms]) for height, terms in parts]
    rows = sum(height for height, _ in heights)
    return pl.pallas_call(
        functools.partial(combine_kernel, heights),
        out_shape=jax.ShapeDtypeStruct((rows, arrays[0].shape[1]), arrays[0].dtype),
        compiler_params=pltpu.CompilerParams(vmem_limit_bytes=16 * MIB),
        name="combine_rows",
    )(*arrays)


def local(ring, hidden_in, norm_gain, router_weight, expert_ids, w_gate, w_up, w_down):
    rows = hidden_in.shape[0]
    num_experts = router_weight.shape[1]
    local_experts = w_gate.shape[0]
    chips = len(ring)
    full, half = chips // 2 - 1, rows // 2
    tie = lax.optimization_barrier

    def shift(by):
        pairs = [
            (2 * ring[p] + c, 2 * ring[(p + by) % chips] + c)
            for p in range(chips)
            for c in range(2)
        ]
        return lambda x: lax.ppermute(x, "expert", pairs)

    ahead, behind = shift(1), shift(-1)

    def sibling(x):
        return lax.ppermute(x, "expert", [(d, d ^ 1) for d in range(2 * chips)])

    packed, first, second = pack(hidden_in, norm_gain, router_weight, expert_ids)
    lane = jnp.arange(packed.shape[1] - hidden_in.shape[1], dtype=jnp.int32)[None, :]
    place = lax.axis_index("expert")

    here = place * local_experts + jnp.arange(local_experts, dtype=jnp.int32)[:, None]
    mine = ((lane == here) | (lane == num_experts + here)).astype(jnp.float32)

    def run(shards, splits):
        total = None
        for e in range(local_experts):
            outs = ffn(shards, splits, w_gate[e], w_up[e], w_down[e], mine[e : e + 1])
            if total is None:
                total = outs
            else:
                total = [combine((a.shape[0], [(a, 0), (b, 0)])) for a, b in zip(total, outs)]
        return total

    def near(ours, theirs, count):
        return run([ours, theirs], [half] * count + [half * count])

    mine = beside_weights(mine, w_gate, w_up, w_down)
    long_a, long_b, short_a, short_b = [first], [second], [first], [second]
    terms, came = [None] * (full + 1), [None] * (full + 1)

    def beside(hops, k):
        if k < 1:
            return hops
        ours = join([long_a[k], short_b[k], short_a[k], long_b[k]])
        *terms[k], sent = near(ours, sibling(ours), 4)
        *hops, sent = tie((*hops, sent))
        came[k] = sibling(sent)
        return hops

    for k in range(1, full + 2):
        long_a.append(ahead(long_a[-1]))
        long_b.append(behind(long_b[-1]))
        if k <= full:
            short_a.append(behind(short_a[-1]))
            short_b.append(ahead(short_b[-1]))
        if k == 1:
            long_a[1], long_b[1], mine = tie((long_a[1], long_b[1], mine))
            own_kept, sent = run([packed, sibling(packed)], [rows, rows])
        elif k == 2:
            long_a[2], long_b[2], sent = tie((long_a[2], long_b[2], sent))
            own_came = sibling(sent)
        else:
            long_a[k], long_b[k] = beside((long_a[k], long_b[k]), k - 2 if k <= full else full)
    far = join([long_a[-1], long_b[-1]])
    far_a, far_b, sent = near(far, sibling(far), 2)

    def part(k, i, *more):
        return combine((half, [(terms[k][i], 0), (came[k], i * half), *((m, 0) for m in more)]))

    by_short_b, by_short_a = behind(part(full, 1)), ahead(part(full, 2))
    far_came = sibling(sent)
    by_long_a = behind(combine((half, [(far_a, 0), (far_came, 0)])))
    by_long_b = ahead(combine((half, [(far_b, 0), (far_came, half)])))
    by_long_a, by_long_b, by_short_a, by_short_b = beside(
        (by_long_a, by_long_b, by_short_a, by_short_b), full - 1
    )
    for k in range(full, 0, -1):
        by_long_a, by_long_b = behind(part(k, 0, by_long_a)), ahead(part(k, 3, by_long_b))
        if k > 1:
            by_short_b, by_short_a = (
                behind(part(k - 1, 1, by_short_b)),
                ahead(part(k - 1, 2, by_short_a)),
            )
    return combine(
        (half, [(own_kept, 0), (own_came, 0), (by_long_a, 0), (by_short_a, 0)]),
        (half, [(own_kept, half), (own_came, half), (by_long_b, 0), (by_short_b, 0)]),
    )


def solution(mesh):
    in_specs = (
        P(("groups", "expert"), None),
        P(),
        P(),
        P(("groups", "expert"), None),
        P("expert", None, None),
        P("expert", None, None),
        P("expert", None, None),
    )
    out_specs = P(("groups", "expert"), None)
    chips = mesh.shape["expert"] // 2
    columns = max(1, 4 // mesh.shape["groups"])
    if columns == 2 and chips % 2 == 0:
        ring = list(range(0, chips, 2)) + list(range(chips - 1, 0, -2))
    else:
        ring = list(range(chips))
    return jax.shard_map(
        functools.partial(local, ring),
        mesh=mesh,
        in_specs=in_specs,
        out_specs=out_specs,
        check_vma=False,
    )
```

profile of v0, /device:TPU:0, one launch (start us, length us, event | category | flops | bytes accessed | tf_op | source)
XLA Modules:
  0.0 114.1 jit_solution(4633045817395459893)
XLA Ops:
  0.0 2.6 %pack_rows.1 = (bf16[128,2176]{1,0:T(8,128)(2,1)}, bf16[64,2176]{1,0:T(8,128)(2,1)}, bf16[64,2176]{1,0:T(8,128)(2,1)}) custom-call(bf16[128,2048]{1,0:T(8,128)(2,1)} %refs_0_.2, f32[1,2048]{1,0:T(1,128)} %bitcast.22, bf16[16,2048]{1,0:T(8,128)(2,1)} %bitcast.21, s32[8,128]{1,0:T(8,128)} %bitcast.23), custom_call_target="tpu_custom_call" | custom-call | tf_op jit(solution)/shard_map/pack_rows/pallas_call | solution.py:57
  2.6 3.1 %collective-permute-start.1 = (bf16[64,2176]{1,0:T(8,128)(2,1)}, bf16[64,2176]{1,0:T(8,128)(2,1)S(1)}, u32[]{:S(2)}, u32[]{:S(2)}) collective-permute-start(bf16[64,2176]{1,0:T(8,128)(2,1)} %get-tuple-element.46), channel_id=1, source_target_pairs={{0,4},{1,5},{4,8},{5,9},{8,12},{9,13},{12,14},{13,15},{14,10},{15,... | collective-permute-start | bytes 835592 | tf_op jit(solution)/shard_map/ppermute | solution.py:198
  5.7 2.0 %collective-permute-start.6 = (bf16[64,2176]{1,0:T(8,128)(2,1)}, bf16[64,2176]{1,0:T(8,128)(2,1)S(1)}, u32[]{:S(2)}, u32[]{:S(2)}) collective-permute-start(bf16[64,2176]{1,0:T(8,128)(2,1)} %get-tuple-element.47), channel_id=1, source_target_pairs={{0,4},{1,5},{4,8},{5,9},{8,12},{9,13},{12,14},{13,15},{14,10},{15,... | collective-permute-start | bytes 835592 | tf_op jit(solution)/shard_map/ppermute | solution.py:198
  7.8 1.9 %copy-done = bf16[1,2048,768]{2,1,0:T(8,128)(2,1)S(1)} copy-done((bf16[1,2048,768]{2,1,0:T(8,128)(2,1)S(1)}, bf16[1,2048,768]{2,1,0:T(8,128)(2,1)}, u32[]{:S(2)}) %copy-start) | copy-done | bytes 3145752
  9.6 1.9 %copy-done.2 = bf16[1,2048,768]{2,1,0:T(8,128)(2,1)S(1)} copy-done((bf16[1,2048,768]{2,1,0:T(8,128)(2,1)S(1)}, bf16[1,2048,768]{2,1,0:T(8,128)(2,1)}, u32[]{:S(2)}) %copy-start.2) | copy-done | bytes 3145752
  11.5 1.9 %copy-done.4 = bf16[1,768,2048]{2,1,0:T(8,128)(2,1)S(1)} copy-done((bf16[1,768,2048]{2,1,0:T(8,128)(2,1)S(1)}, bf16[1,768,2048]{2,1,0:T(8,128)(2,1)}, u32[]{:S(2)}) %copy-start.4) | copy-done | bytes 3145752
  13.4 2.1 %collective-permute-done.2.refs_3_ = bf16[64,2176]{1,0:T(8,128)(2,1)S(1)} collective-permute-done((bf16[64,2176]{1,0:T(8,128)(2,1)}, bf16[64,2176]{1,0:T(8,128)(2,1)S(1)}, u32[]{:S(2)}, u32[]{:S(2)}) %collective-permute-start.2) | collective-permute-done | bytes 278560 | tf_op jit(solution)/shard_map/ppermute | solution.py:198
  15.5 3.0 %collective-permute-done.6.refs_1_ = bf16[64,2176]{1,0:T(8,128)(2,1)S(1)} collective-permute-done((bf16[64,2176]{1,0:T(8,128)(2,1)}, bf16[64,2176]{1,0:T(8,128)(2,1)S(1)}, u32[]{:S(2)}, u32[]{:S(2)}) %collective-permute-start.6) | collective-permute-done | bytes 278560 | tf_op jit(solution)/shard_map/ppermute | solution.py:198
  20.7 1.6 %collective-permute-start.3 = (bf16[64,2176]{1,0:T(8,128)(2,1)S(1)}, bf16[64,2176]{1,0:T(8,128)(2,1)S(1)}, u32[]{:S(2)}, u32[]{:S(2)}) collective-permute-start(bf16[64,2176]{1,0:T(8,128)(2,1)S(1)} %collective-permute-done.1.refs_0_), channel_id=1, source_target_pairs={{0,4},{1,5},{4,8},{5,9},{8,12},{9,13},{12,14},{13,15},{14,10},{15,... | collective-permute-start | bytes 835592 | tf_op jit(solution)/shard_map/ppermute | solution.py:198
  22.7 1.6 %collective-permute-start.12 = (bf16[64,2176]{1,0:T(8,128)(2,1)S(1)}, bf16[64,2176]{1,0:T(8,128)(2,1)S(1)}, u32[]{:S(2)}, u32[]{:S(2)}) collective-permute-start(bf16[64,2176]{1,0:T(8,128)(2,1)S(1)} %collective-permute-done.6.refs_1_), channel_id=1, source_target_pairs={{0,4},{1,5},{4,8},{5,9},{8,12},{9,13},{12,14},{13,15},{14,10},{15,... | collective-permute-start | bytes 835592 | tf_op jit(solution)/shard_map/ppermute | solution.py:198
  24.7 3.9 %expert_ffn.5 = (bf16[128,2048]{1,0:T(8,128)(2,1)S(1)}, bf16[128,2048]{1,0:T(8,128)(2,1)S(1)}) custom-call(bf16[128,2176]{1,0:T(8,128)(2,1)S(1)} %copy-done.5, bf16[128,2176]{1,0:T(8,128)(2,1)S(1)} %collective-permute-done.refs_1_, bf16[2048,768]{1,0:T(8,128)(2,1)S(1)} %bitcast.6, bf16[2048,768]{1,0:T(8,128)(2,1)S(1)} %bitcast.11, ...), custom_call_target="tpu_custom_call" | custom-call | flops 2415919104 | bytes 524288 | tf_op jit(solution)/shard_map/expert_ffn/pallas_call | solution.py:111
  30.2 1.6 %collective-permute-done.4.refs_3_ = bf16[64,2176]{1,0:T(8,128)(2,1)S(1)} collective-permute-done((bf16[64,2176]{1,0:T(8,128)(2,1)S(1)}, bf16[64,2176]{1,0:T(8,128)(2,1)S(1)}, u32[]{:S(2)}, u32[]{:S(2)}) %collective-permute-start.4) | collective-permute-done | bytes 278560 | tf_op jit(solution)/shard_map/ppermute | solution.py:198
  32.2 1.6 %collective-permute-start.9 = (bf16[64,2176]{1,0:T(8,128)(2,1)S(1)}, bf16[64,2176]{1,0:T(8,128)(2,1)S(1)}, u32[]{:S(2)}, u32[]{:S(2)}) collective-permute-start(bf16[64,2176]{1,0:T(8,128)(2,1)S(1)} %collective-permute-done.3.refs_0_), channel_id=1, source_target_pairs={{0,4},{1,5},{4,8},{5,9},{8,12},{9,13},{12,14},{13,15},{14,10},{15,... | collective-permute-start | bytes 835592 | tf_op jit(solution)/shard_map/ppermute | solution.py:198
  33.8 2.3 %collective-permute-done.12.refs_1_ = bf16[64,2176]{1,0:T(8,128)(2,1)S(1)} collective-permute-done((bf16[64,2176]{1,0:T(8,128)(2,1)S(1)}, bf16[64,2176]{1,0:T(8,128)(2,1)S(1)}, u32[]{:S(2)}, u32[]{:S(2)}) %collective-permute-start.12) | collective-permute-done | bytes 278560 | tf_op jit(solution)/shard_map/ppermute | solution.py:198
  38.2 6.4 %expert_ffn.6 = (bf16[64,2048]{1,0:T(8,128)(2,1)S(1)}, bf16[64,2048]{1,0:T(8,128)(2,1)S(1)}, bf16[64,2048]{1,0:T(8,128)(2,1)S(1)}, bf16[64,2048]{1,0:T(8,128)(2,1)S(1)}, bf16[256,2048]{1,0:T(8,128)(2,1)S(1)}) custom-call(bf16[256,2176]{1,0:T(8,128)(2,1)S(1)} %join_rows.4.refs_0_, bf16[256,2176]{1,0:T(8,128)(2,1)S(1)} %collective-permute-done.8.refs_1_, ...), custom_call_target="tpu_custom_call" | custom-call | flops 4831838208 | bytes 1048576 | tf_op jit(solution)/shard_map/expert_ffn/pallas_call | solution.py:111
  44.6 2.6 %collective-permute-done.17.refs_1_ = bf16[64,2176]{1,0:T(8,128)(2,1)S(1)} collective-permute-done((bf16[64,2176]{1,0:T(8,128)(2,1)S(1)}, bf16[64,2176]{1,0:T(8,128)(2,1)S(1)}, u32[]{:S(2)}, u32[]{:S(2)}) %collective-permute-start.17) | collective-permute-done | bytes 278560 | tf_op jit(solution)/shard_map/ppermute | solution.py:198
  48.7 1.6 %collective-permute-start.15 = (bf16[64,2176]{1,0:T(8,128)(2,1)S(1)}, bf16[64,2176]{1,0:T(8,128)(2,1)S(1)}, u32[]{:S(2)}, u32[]{:S(2)}) collective-permute-start(bf16[64,2176]{1,0:T(8,128)(2,1)S(1)} %collective-permute-done.9.refs_0_), channel_id=1, source_target_pairs={{0,4},{1,5},{4,8},{5,9},{8,12},{9,13},{12,14},{13,15},{14,10},{15,... | collective-permute-start | bytes 835592 | tf_op jit(solution)/shard_map/ppermute | solution.py:198
  51.4 6.4 %expert_ffn.8 = (bf16[64,2048]{1,0:T(8,128)(2,1)S(1)}, bf16[64,2048]{1,0:T(8,128)(2,1)S(1)}, bf16[64,2048]{1,0:T(8,128)(2,1)S(1)}, bf16[64,2048]{1,0:T(8,128)(2,1)S(1)}, bf16[256,2048]{1,0:T(8,128)(2,1)S(1)}) custom-call(bf16[256,2176]{1,0:T(8,128)(2,1)S(1)} %join_rows.6.refs_0_, bf16[256,2176]{1,0:T(8,128)(2,1)S(1)} %collective-permute-done.19.refs_1_, ...), custom_call_target="tpu_custom_call" | custom-call | flops 4831838208 | bytes 1048576 | tf_op jit(solution)/shard_map/expert_ffn/pallas_call | solution.py:111
  61.1 3.9 %expert_ffn.9 = (bf16[64,2048]{1,0:T(8,128)(2,1)S(1)}, bf16[64,2048]{1,0:T(8,128)(2,1)S(1)}, bf16[128,2048]{1,0:T(8,128)(2,1)S(1)}) custom-call(bf16[128,2176]{1,0:T(8,128)(2,1)S(1)} %join_rows.7.refs_0_, bf16[128,2176]{1,0:T(8,128)(2,1)S(1)} %collective-permute-done.20.refs_1_, bf16[2048,768]{1,0:T(8,128)(2,1)S(1)} %bitcast.9, ...), custom_call_target="tpu_custom_call" | custom-call | flops 2415919104 | bytes 524288 | tf_op jit(solution)/shard_map/expert_ffn/pallas_call | solution.py:111
  65.9 1.6 %collective-permute-start.25 = (bf16[64,2048]{1,0:T(8,128)(2,1)S(1)}, bf16[64,2048]{1,0:T(8,128)(2,1)S(1)}, u32[]{:S(2)}, u32[]{:S(2)}) collective-permute-start(bf16[64,2048]{1,0:T(8,128)(2,1)S(1)} %combine_rows.17), channel_id=1, source_target_pairs={{0,4},{1,5},{4,8},{5,9},{8,12},{9,13},{12,14},{13,15},{14,10},{15,... | collective-permute-start | bytes 786440 | tf_op jit(solution)/shard_map/ppermute | solution.py:198
  67.6 1.6 %collective-permute-start.23 = (bf16[64,2048]{1,0:T(8,128)(2,1)S(1)}, bf16[64,2048]{1,0:T(8,128)(2,1)S(1)}, u32[]{:S(2)}, u32[]{:S(2)}) collective-permute-start(bf16[64,2048]{1,0:T(8,128)(2,1)S(1)} %combine_rows.16), channel_id=1, source_target_pairs={{0,4},{1,5},{4,8},{5,9},{8,12},{9,13},{12,14},{13,15},{14,10},{15,... | collective-permute-start | bytes 786440 | tf_op jit(solution)/shard_map/ppermute | solution.py:198
  69.8 6.4 %expert_ffn.7 = (bf16[64,2048]{1,0:T(8,128)(2,1)S(1)}, bf16[64,2048]{1,0:T(8,128)(2,1)S(1)}, bf16[64,2048]{1,0:T(8,128)(2,1)S(1)}, bf16[64,2048]{1,0:T(8,128)(2,1)S(1)}, bf16[256,2048]{1,0:T(8,128)(2,1)S(1)}) custom-call(bf16[256,2176]{1,0:T(8,128)(2,1)S(1)} %join_rows.5.refs_0_, bf16[256,2176]{1,0:T(8,128)(2,1)S(1)} %collective-permute-done.14.refs_1_, ...), custom_call_target="tpu_custom_call" | custom-call | flops 4831838208 | bytes 1048576 | tf_op jit(solution)/shard_map/expert_ffn/pallas_call | solution.py:111
  76.2 3.7 %collective-permute-done.23.refs_2_ = bf16[64,2048]{1,0:T(8,128)(2,1)S(1)} collective-permute-done((bf16[64,2048]{1,0:T(8,128)(2,1)S(1)}, bf16[64,2048]{1,0:T(8,128)(2,1)S(1)}, u32[]{:S(2)}, u32[]{:S(2)}) %collective-permute-start.23) | collective-permute-done | bytes 262176 | tf_op jit(solution)/shard_map/ppermute | solution.py:198
  80.4 1.6 %collective-permute-start.33 = (bf16[64,2048]{1,0:T(8,128)(2,1)S(1)}, bf16[64,2048]{1,0:T(8,128)(2,1)S(1)}, u32[]{:S(2)}, u32[]{:S(2)}) collective-permute-start(bf16[64,2048]{1,0:T(8,128)(2,1)S(1)} %combine_rows.24), channel_id=1, source_target_pairs={{0,4},{1,5},{4,8},{5,9},{8,12},{9,13},{12,14},{13,15},{14,10},{15,... | collective-permute-start | bytes 786440 | tf_op jit(solution)/shard_map/ppermute | solution.py:198
  83.3 5.4 %collective-permute-done.33.refs_2_ = bf16[64,2048]{1,0:T(8,128)(2,1)S(1)} collective-permute-done((bf16[64,2048]{1,0:T(8,128)(2,1)S(1)}, bf16[64,2048]{1,0:T(8,128)(2,1)S(1)}, u32[]{:S(2)}, u32[]{:S(2)}) %collective-permute-start.33) | collective-permute-done | bytes 262176 | tf_op jit(solution)/shard_map/ppermute | solution.py:198
  88.8 1.6 %collective-permute-start.34 = (bf16[64,2048]{1,0:T(8,128)(2,1)S(1)}, bf16[64,2048]{1,0:T(8,128)(2,1)S(1)}, u32[]{:S(2)}, u32[]{:S(2)}) collective-permute-start(bf16[64,2048]{1,0:T(8,128)(2,1)S(1)} %combine_rows.25), channel_id=1, source_target_pairs={{0,4},{1,5},{4,8},{5,9},{8,12},{9,13},{12,14},{13,15},{14,10},{15,... | collective-permute-start | bytes 786440 | tf_op jit(solution)/shard_map/ppermute | solution.py:198
  93.6 3.4 %collective-permute-done.36.refs_2_ = bf16[64,2048]{1,0:T(8,128)(2,1)S(1)} collective-permute-done((bf16[64,2048]{1,0:T(8,128)(2,1)S(1)}, bf16[64,2048]{1,0:T(8,128)(2,1)S(1)}, u32[]{:S(2)}, u32[]{:S(2)}) %collective-permute-start.36) | collective-permute-done | bytes 262176 | tf_op jit(solution)/shard_map/ppermute | solution.py:198
  98.2 1.6 %collective-permute-start.35 = (bf16[64,2048]{1,0:T(8,128)(2,1)S(1)}, bf16[64,2048]{1,0:T(8,128)(2,1)S(1)}, u32[]{:S(2)}, u32[]{:S(2)}) collective-permute-start(bf16[64,2048]{1,0:T(8,128)(2,1)S(1)} %combine_rows.26), channel_id=1, source_target_pairs={{0,4},{1,5},{4,8},{5,9},{8,12},{9,13},{12,14},{13,15},{14,10},{15,... | collective-permute-start | bytes 786440 | tf_op jit(solution)/shard_map/ppermute | solution.py:198
  99.8 3.9 %collective-permute-done.31.refs_2_ = bf16[64,2048]{1,0:T(8,128)(2,1)S(1)} collective-permute-done((bf16[64,2048]{1,0:T(8,128)(2,1)S(1)}, bf16[64,2048]{1,0:T(8,128)(2,1)S(1)}, u32[]{:S(2)}, u32[]{:S(2)}) %collective-permute-start.31) | collective-permute-done | bytes 262176 | tf_op jit(solution)/shard_map/ppermute | solution.py:198
  103.8 1.6 %collective-permute-start.32 = (bf16[64,2048]{1,0:T(8,128)(2,1)S(1)}, bf16[64,2048]{1,0:T(8,128)(2,1)S(1)}, u32[]{:S(2)}, u32[]{:S(2)}) collective-permute-start(bf16[64,2048]{1,0:T(8,128)(2,1)S(1)} %combine_rows.23), channel_id=1, source_target_pairs={{0,4},{1,5},{4,8},{5,9},{8,12},{9,13},{12,14},{13,15},{14,10},{15,... | collective-permute-start | bytes 786440 | tf_op jit(solution)/shard_map/ppermute | solution.py:198
  106.1 2.2 %collective-permute-done.37.refs_7_ = bf16[64,2048]{1,0:T(8,128)(2,1)S(1)} collective-permute-done((bf16[64,2048]{1,0:T(8,128)(2,1)S(1)}, bf16[64,2048]{1,0:T(8,128)(2,1)S(1)}, u32[]{:S(2)}, u32[]{:S(2)}) %collective-permute-start.37) | collective-permute-done | bytes 262176 | tf_op jit(solution)/shard_map/ppermute | solution.py:198
  109.3 3.7 %collective-permute-done.32.refs_3_ = bf16[64,2048]{1,0:T(8,128)(2,1)S(1)} collective-permute-done((bf16[64,2048]{1,0:T(8,128)(2,1)S(1)}, bf16[64,2048]{1,0:T(8,128)(2,1)S(1)}, u32[]{:S(2)}, u32[]{:S(2)}) %collective-permute-start.32) | collective-permute-done | bytes 262176 | tf_op jit(solution)/shard_map/ppermute | solution.py:198
  (83 shorter events, 23.5 us)
Async XLA Ops:
  2.6 10.8 %collective-permute-start.1 = (bf16[64,2176]{1,0:T(8,128)(2,1)}, bf16[64,2176]{1,0:T(8,128)(2,1)S(1)}, u32[]{:S(2)}, u32[]{:S(2)}) collective-permute-start(bf16[64,2176]{1,0:T(8,128)(2,1)} %get-tuple-element.46), channel_id=1, source_target_pairs={{0,4},{1,5},{4,8},{5,9},{8,12},{9,13},{12,14},{13,15},{14,10},{15,... | collective-permute-start | bytes 835592 | tf_op jit(solution)/shard_map/ppermute | solution.py:198
  5.7 9.8 %collective-permute-start.2 = (bf16[64,2176]{1,0:T(8,128)(2,1)}, bf16[64,2176]{1,0:T(8,128)(2,1)S(1)}, u32[]{:S(2)}, u32[]{:S(2)}) collective-permute-start(bf16[64,2176]{1,0:T(8,128)(2,1)} %get-tuple-element.47), channel_id=1, source_target_pairs={{0,2},{1,3},{4,0},{5,1},{8,4},{9,5},{12,8},{13,9},{14,12},{15,13},... | collective-permute-start | bytes 835592 | tf_op jit(solution)/shard_map/ppermute | solution.py:198
  5.7 12.8 %collective-permute-start.6 = (bf16[64,2176]{1,0:T(8,128)(2,1)}, bf16[64,2176]{1,0:T(8,128)(2,1)S(1)}, u32[]{:S(2)}, u32[]{:S(2)}) collective-permute-start(bf16[64,2176]{1,0:T(8,128)(2,1)} %get-tuple-element.47), channel_id=1, source_target_pairs={{0,4},{1,5},{4,8},{5,9},{8,12},{9,13},{12,14},{13,15},{14,10},{15,... | collective-permute-start | bytes 835592 | tf_op jit(solution)/shard_map/ppermute | solution.py:198
  7.7 12.3 %collective-permute-start.7 = (bf16[64,2176]{1,0:T(8,128)(2,1)}, bf16[64,2176]{1,0:T(8,128)(2,1)S(1)}, u32[]{:S(2)}, u32[]{:S(2)}) collective-permute-start(bf16[64,2176]{1,0:T(8,128)(2,1)} %get-tuple-element.46), channel_id=1, source_target_pairs={{0,2},{1,3},{4,0},{5,1},{8,4},{9,5},{12,8},{13,9},{14,12},{15,13},... | collective-permute-start | bytes 835592 | tf_op jit(solution)/shard_map/ppermute | solution.py:198
  20.1 18.1 %collective-permute-start.8 = (bf16[256,2176]{1,0:T(8,128)(2,1)S(1)}, bf16[256,2176]{1,0:T(8,128)(2,1)S(1)}, u32[]{:S(2)}, u32[]{:S(2)}) collective-permute-start(bf16[256,2176]{1,0:T(8,128)(2,1)S(1)} %join_rows.4.refs_0_), channel_id=1, source_target_pairs={{0,1},{1,0},{2,3},{3,2},{4,5},{5,4},{6,7},{7,6},{8,9},{9,8},{10,11... | collective-permute-start | bytes 3342344 | tf_op jit(solution)/shard_map/ppermute | solution.py:203
  20.7 9.5 %collective-permute-start.3 = (bf16[64,2176]{1,0:T(8,128)(2,1)S(1)}, bf16[64,2176]{1,0:T(8,128)(2,1)S(1)}, u32[]{:S(2)}, u32[]{:S(2)}) collective-permute-start(bf16[64,2176]{1,0:T(8,128)(2,1)S(1)} %collective-permute-done.1.refs_0_), channel_id=1, source_target_pairs={{0,4},{1,5},{4,8},{5,9},{8,12},{9,13},{12,14},{13,15},{14,10},{15,... | collective-permute-start | bytes 835592 | tf_op jit(solution)/shard_map/ppermute | solution.py:198
  22.2 9.6 %collective-permute-start.4 = (bf16[64,2176]{1,0:T(8,128)(2,1)S(1)}, bf16[64,2176]{1,0:T(8,128)(2,1)S(1)}, u32[]{:S(2)}, u32[]{:S(2)}) collective-permute-start(bf16[64,2176]{1,0:T(8,128)(2,1)S(1)} %collective-permute-done.2.refs_3_), channel_id=1, source_target_pairs={{0,2},{1,3},{4,0},{5,1},{8,4},{9,5},{12,8},{13,9},{14,12},{15,13},... | collective-permute-start | bytes 835592 | tf_op jit(solution)/shard_map/ppermute | solution.py:198
  22.7 13.5 %collective-permute-start.12 = (bf16[64,2176]{1,0:T(8,128)(2,1)S(1)}, bf16[64,2176]{1,0:T(8,128)(2,1)S(1)}, u32[]{:S(2)}, u32[]{:S(2)}) collective-permute-start(bf16[64,2176]{1,0:T(8,128)(2,1)S(1)} %collective-permute-done.6.refs_1_), channel_id=1, source_target_pairs={{0,4},{1,5},{4,8},{5,9},{8,12},{9,13},{12,14},{13,15},{14,10},{15,... | collective-permute-start | bytes 835592 | tf_op jit(solution)/shard_map/ppermute | solution.py:198
  24.3 13.5 %collective-permute-start.13 = (bf16[64,2176]{1,0:T(8,128)(2,1)S(1)}, bf16[64,2176]{1,0:T(8,128)(2,1)S(1)}, u32[]{:S(2)}, u32[]{:S(2)}) collective-permute-start(bf16[64,2176]{1,0:T(8,128)(2,1)S(1)} %collective-permute-done.7.refs_2_), channel_id=1, source_target_pairs={{0,2},{1,3},{4,0},{5,1},{8,4},{9,5},{12,8},{13,9},{14,12},{15,13},... | collective-permute-start | bytes 835592 | tf_op jit(solution)/shard_map/ppermute | solution.py:198
  31.8 12.8 %collective-permute-start.10 = (bf16[64,2176]{1,0:T(8,128)(2,1)S(1)}, bf16[64,2176]{1,0:T(8,128)(2,1)S(1)}, u32[]{:S(2)}, u32[]{:S(2)}) collective-permute-start(bf16[64,2176]{1,0:T(8,128)(2,1)S(1)} %collective-permute-done.4.refs_3_), channel_id=1, source_target_pairs={{0,2},{1,3},{4,0},{5,1},{8,4},{9,5},{12,8},{13,9},{14,12},{15,13},... | collective-permute-start | bytes 835592 | tf_op jit(solution)/shard_map/ppermute | solution.py:198
  32.2 12.4 %collective-permute-start.9 = (bf16[64,2176]{1,0:T(8,128)(2,1)S(1)}, bf16[64,2176]{1,0:T(8,128)(2,1)S(1)}, u32[]{:S(2)}, u32[]{:S(2)}) collective-permute-start(bf16[64,2176]{1,0:T(8,128)(2,1)S(1)} %collective-permute-done.3.refs_0_), channel_id=1, source_target_pairs={{0,4},{1,5},{4,8},{5,9},{8,12},{9,13},{12,14},{13,15},{14,10},{15,... | collective-permute-start | bytes 835592 | tf_op jit(solution)/shard_map/ppermute | solution.py:198
  36.1 11.1 %collective-permute-start.17 = (bf16[64,2176]{1,0:T(8,128)(2,1)S(1)}, bf16[64,2176]{1,0:T(8,128)(2,1)S(1)}, u32[]{:S(2)}, u32[]{:S(2)}) collective-permute-start(bf16[64,2176]{1,0:T(8,128)(2,1)S(1)} %collective-permute-done.12.refs_1_), channel_id=1, source_target_pairs={{0,4},{1,5},{4,8},{5,9},{8,12},{9,13},{12,14},{13,15},{14,10},{15,... | collective-permute-start | bytes 835592 | tf_op jit(solution)/shard_map/ppermute | solution.py:198
  37.8 10.8 %collective-permute-start.18 = (bf16[64,2176]{1,0:T(8,128)(2,1)S(1)}, bf16[64,2176]{1,0:T(8,128)(2,1)S(1)}, u32[]{:S(2)}, u32[]{:S(2)}) collective-permute-start(bf16[64,2176]{1,0:T(8,128)(2,1)S(1)} %collective-permute-done.13.refs_2_), channel_id=1, source_target_pairs={{0,2},{1,3},{4,0},{5,1},{8,4},{9,5},{12,8},{13,9},{14,12},{15,13},... | collective-permute-start | bytes 835592 | tf_op jit(solution)/shard_map/ppermute | solution.py:198
  48.7 9.1 %collective-permute-start.15 = (bf16[64,2176]{1,0:T(8,128)(2,1)S(1)}, bf16[64,2176]{1,0:T(8,128)(2,1)S(1)}, u32[]{:S(2)}, u32[]{:S(2)}) collective-permute-start(bf16[64,2176]{1,0:T(8,128)(2,1)S(1)} %collective-permute-done.9.refs_0_), channel_id=1, source_target_pairs={{0,4},{1,5},{4,8},{5,9},{8,12},{9,13},{12,14},{13,15},{14,10},{15,... | collective-permute-start | bytes 835592 | tf_op jit(solution)/shard_map/ppermute | solution.py:198
  50.3 8.7 %collective-permute-start.16 = (bf16[64,2176]{1,0:T(8,128)(2,1)S(1)}, bf16[64,2176]{1,0:T(8,128)(2,1)S(1)}, u32[]{:S(2)}, u32[]{:S(2)}) collective-permute-start(bf16[64,2176]{1,0:T(8,128)(2,1)S(1)} %collective-permute-done.10.refs_3_), channel_id=1, source_target_pairs={{0,2},{1,3},{4,0},{5,1},{8,4},{9,5},{12,8},{13,9},{14,12},{15,13},... | collective-permute-start | bytes 835592 | tf_op jit(solution)/shard_map/ppermute | solution.py:198
  59.2 10.5 %collective-permute-start.14 = (bf16[256,2176]{1,0:T(8,128)(2,1)S(1)}, bf16[256,2176]{1,0:T(8,128)(2,1)S(1)}, u32[]{:S(2)}, u32[]{:S(2)}) collective-permute-start(bf16[256,2176]{1,0:T(8,128)(2,1)S(1)} %join_rows.5.refs_0_), channel_id=1, source_target_pairs={{0,1},{1,0},{2,3},{3,2},{4,5},{5,4},{6,7},{7,6},{8,9},{9,8},{10,11... | collective-permute-start | bytes 3342344 | tf_op jit(solution)/shard_map/ppermute | solution.py:203
  65.3 10.9 %collective-permute-start.26 = (bf16[64,2048]{1,0:T(8,128)(2,1)S(1)}, bf16[64,2048]{1,0:T(8,128)(2,1)S(1)}, u32[]{:S(2)}, u32[]{:S(2)}) collective-permute-start(bf16[64,2048]{1,0:T(8,128)(2,1)S(1)} %combine_rows.18), channel_id=1, source_target_pairs={{0,2},{1,3},{4,0},{5,1},{8,4},{9,5},{12,8},{13,9},{14,12},{15,13},... | collective-permute-start | bytes 786440 | tf_op jit(solution)/shard_map/ppermute | solution.py:198
  65.9 10.3 %collective-permute-start.25 = (bf16[64,2048]{1,0:T(8,128)(2,1)S(1)}, bf16[64,2048]{1,0:T(8,128)(2,1)S(1)}, u32[]{:S(2)}, u32[]{:S(2)}) collective-permute-start(bf16[64,2048]{1,0:T(8,128)(2,1)S(1)} %combine_rows.17), channel_id=1, source_target_pairs={{0,4},{1,5},{4,8},{5,9},{8,12},{9,13},{12,14},{13,15},{14,10},{15,... | collective-permute-start | bytes 786440 | tf_op jit(solution)/shard_map/ppermute | solution.py:198
  67.6 12.3 %collective-permute-start.23 = (bf16[64,2048]{1,0:T(8,128)(2,1)S(1)}, bf16[64,2048]{1,0:T(8,128)(2,1)S(1)}, u32[]{:S(2)}, u32[]{:S(2)}) collective-permute-start(bf16[64,2048]{1,0:T(8,128)(2,1)S(1)} %combine_rows.16), channel_id=1, source_target_pairs={{0,4},{1,5},{4,8},{5,9},{8,12},{9,13},{12,14},{13,15},{14,10},{15,... | collective-permute-start | bytes 786440 | tf_op jit(solution)/shard_map/ppermute | solution.py:198
  69.2 10.6 %collective-permute-start.22 = (bf16[64,2048]{1,0:T(8,128)(2,1)S(1)}, bf16[64,2048]{1,0:T(8,128)(2,1)S(1)}, u32[]{:S(2)}, u32[]{:S(2)}) collective-permute-start(bf16[64,2048]{1,0:T(8,128)(2,1)S(1)} %combine_rows.15), channel_id=1, source_target_pairs={{0,2},{1,3},{4,0},{5,1},{8,4},{9,5},{12,8},{13,9},{14,12},{15,13},... | collective-permute-start | bytes 786440 | tf_op jit(solution)/shard_map/ppermute | solution.py:198
  79.8 13.2 %collective-permute-start.11 = (bf16[256,2048]{1,0:T(8,128)(2,1)S(1)}, bf16[256,2048]{1,0:T(8,128)(2,1)S(1)}, u32[]{:S(2)}, u32[]{:S(2)}) collective-permute-start(bf16[256,2048]{1,0:T(8,128)(2,1)S(1)} %get-tuple-element.58), channel_id=1, source_target_pairs={{0,1},{1,0},{2,3},{3,2},{4,5},{5,4},{6,7},{7,6},{8,9},{9,8},{10,11... | collective-permute-start | bytes 3145736 | tf_op jit(solution)/shard_map/ppermute | solution.py:203
  80.4 8.3 %collective-permute-start.33 = (bf16[64,2048]{1,0:T(8,128)(2,1)S(1)}, bf16[64,2048]{1,0:T(8,128)(2,1)S(1)}, u32[]{:S(2)}, u32[]{:S(2)}) collective-permute-start(bf16[64,2048]{1,0:T(8,128)(2,1)S(1)} %combine_rows.24), channel_id=1, source_target_pairs={{0,4},{1,5},{4,8},{5,9},{8,12},{9,13},{12,14},{13,15},{14,10},{15,... | collective-permute-start | bytes 786440 | tf_op jit(solution)/shard_map/ppermute | solution.py:198
  82.2 9.3 %collective-permute-start.28 = (bf16[64,2048]{1,0:T(8,128)(2,1)S(1)}, bf16[64,2048]{1,0:T(8,128)(2,1)S(1)}, u32[]{:S(2)}, u32[]{:S(2)}) collective-permute-start(bf16[64,2048]{1,0:T(8,128)(2,1)S(1)} %combine_rows.19), channel_id=1, source_target_pairs={{0,2},{1,3},{4,0},{5,1},{8,4},{9,5},{12,8},{13,9},{14,12},{15,13},... | collective-permute-start | bytes 786440 | tf_op jit(solution)/shard_map/ppermute | solution.py:198
  82.7 23.4 %collective-permute-start.5 = (bf16[128,2048]{1,0:T(8,128)(2,1)S(1)}, bf16[128,2048]{1,0:T(8,128)(2,1)S(1)}, u32[]{:S(2)}, u32[]{:S(2)}) collective-permute-start(bf16[128,2048]{1,0:T(8,128)(2,1)S(1)} %get-tuple-element.53), channel_id=1, source_target_pairs={{0,1},{1,0},{2,3},{3,2},{4,5},{5,4},{6,7},{7,6},{8,9},{9,8},{10,11... | collective-permute-start | bytes 1572872 | tf_op jit(solution)/shard_map/ppermute | solution.py:203
  82.8 14.3 %collective-permute-start.36 = (bf16[64,2048]{1,0:T(8,128)(2,1)S(1)}, bf16[64,2048]{1,0:T(8,128)(2,1)S(1)}, u32[]{:S(2)}, u32[]{:S(2)}) collective-permute-start(bf16[64,2048]{1,0:T(8,128)(2,1)S(1)} %combine_rows.27), channel_id=1, source_target_pairs={{0,2},{1,3},{4,0},{5,1},{8,4},{9,5},{12,8},{13,9},{14,12},{15,13},... | collective-permute-start | bytes 786440 | tf_op jit(solution)/shard_map/ppermute | solution.py:198
  88.8 9.3 %collective-permute-start.34 = (bf16[64,2048]{1,0:T(8,128)(2,1)S(1)}, bf16[64,2048]{1,0:T(8,128)(2,1)S(1)}, u32[]{:S(2)}, u32[]{:S(2)}) collective-permute-start(bf16[64,2048]{1,0:T(8,128)(2,1)S(1)} %combine_rows.25), channel_id=1, source_target_pairs={{0,4},{1,5},{4,8},{5,9},{8,12},{9,13},{12,14},{13,15},{14,10},{15,... | collective-permute-start | bytes 786440 | tf_op jit(solution)/shard_map/ppermute | solution.py:198
  91.4 12.3 %collective-permute-start.31 = (bf16[64,2048]{1,0:T(8,128)(2,1)S(1)}, bf16[64,2048]{1,0:T(8,128)(2,1)S(1)}, u32[]{:S(2)}, u32[]{:S(2)}) collective-permute-start(bf16[64,2048]{1,0:T(8,128)(2,1)S(1)} %combine_rows.22), channel_id=1, source_target_pairs={{0,4},{1,5},{4,8},{5,9},{8,12},{9,13},{12,14},{13,15},{14,10},{15,... | collective-permute-start | bytes 786440 | tf_op jit(solution)/shard_map/ppermute | solution.py:198
  93.1 12.4 %collective-permute-start.29 = (bf16[64,2048]{1,0:T(8,128)(2,1)S(1)}, bf16[64,2048]{1,0:T(8,128)(2,1)S(1)}, u32[]{:S(2)}, u32[]{:S(2)}) collective-permute-start(bf16[64,2048]{1,0:T(8,128)(2,1)S(1)} %combine_rows.20), channel_id=1, source_target_pairs={{0,2},{1,3},{4,0},{5,1},{8,4},{9,5},{12,8},{13,9},{14,12},{15,13},... | collective-permute-start | bytes 786440 | tf_op jit(solution)/shard_map/ppermute | solution.py:198
  97.1 11.1 %collective-permute-start.37 = (bf16[64,2048]{1,0:T(8,128)(2,1)S(1)}, bf16[64,2048]{1,0:T(8,128)(2,1)S(1)}, u32[]{:S(2)}, u32[]{:S(2)}) collective-permute-start(bf16[64,2048]{1,0:T(8,128)(2,1)S(1)} %combine_rows.28), channel_id=1, source_target_pairs={{0,2},{1,3},{4,0},{5,1},{8,4},{9,5},{12,8},{13,9},{14,12},{15,13},... | collective-permute-start | bytes 786440 | tf_op jit(solution)/shard_map/ppermute | solution.py:198
  98.2 11.1 %collective-permute-start.35 = (bf16[64,2048]{1,0:T(8,128)(2,1)S(1)}, bf16[64,2048]{1,0:T(8,128)(2,1)S(1)}, u32[]{:S(2)}, u32[]{:S(2)}) collective-permute-start(bf16[64,2048]{1,0:T(8,128)(2,1)S(1)} %combine_rows.26), channel_id=1, source_target_pairs={{0,4},{1,5},{4,8},{5,9},{8,12},{9,13},{12,14},{13,15},{14,10},{15,... | collective-permute-start | bytes 786440 | tf_op jit(solution)/shard_map/ppermute | solution.py:198
  103.8 9.3 %collective-permute-start.32 = (bf16[64,2048]{1,0:T(8,128)(2,1)S(1)}, bf16[64,2048]{1,0:T(8,128)(2,1)S(1)}, u32[]{:S(2)}, u32[]{:S(2)}) collective-permute-start(bf16[64,2048]{1,0:T(8,128)(2,1)S(1)} %combine_rows.23), channel_id=1, source_target_pairs={{0,4},{1,5},{4,8},{5,9},{8,12},{9,13},{12,14},{13,15},{14,10},{15,... | collective-permute-start | bytes 786440 | tf_op jit(solution)/shard_map/ppermute | solution.py:198
  105.5 7.5 %collective-permute-start.30 = (bf16[64,2048]{1,0:T(8,128)(2,1)S(1)}, bf16[64,2048]{1,0:T(8,128)(2,1)S(1)}, u32[]{:S(2)}, u32[]{:S(2)}) collective-permute-start(bf16[64,2048]{1,0:T(8,128)(2,1)S(1)} %combine_rows.21), channel_id=1, source_target_pairs={{0,2},{1,3},{4,0},{5,1},{8,4},{9,5},{12,8},{13,9},{14,12},{15,13},... | collective-permute-start | bytes 786440 | tf_op jit(solution)/shard_map/ppermute | solution.py:198
  (12 other events, 54.7 us)
where the time goes:
time: 114 us
  waiting for transfers between devices  43.8 us (38%)
  starting transfers between devices  32.2 us (28%)
  Pallas kernels  32.1 us (28%)
  local copies, waits for them, and re-layouts  5.68 us (5%)
    ppermute x28, waiting for transfers between devices, shift(): return lambda x: lax.ppermute(x, 'expert', pairs)  41.9 us
    ppermute x28, starting transfers between devices, shift(): return lambda x: lax.ppermute(x, 'expert', pairs)  30.2 us
    pallas_call x5, Pallas kernels, ffn(): pl.pallas_call(functools.partial(ffn_kernel, heights, splits), out_shape=...  27 us
    unnamed x12, local copies, waits for them, and re-layouts  5.68 us
    pallas_call x1, Pallas kernels, pack(): pl.pallas_call(pack_kernel, out_shape=[jax.ShapeDtypeStruct((r, width + l...  2.62 us
  transfers between devices with their start and end apart: 38, of which 20 were waited for; matrix products, arithmetic and copies ran while one was open for 0% of the time, Pallas kernels for 25%

commit v1 on v0

--- a/solution.py
+++ b/solution.py
@@ -248,7 +248,7 @@
             long_a[2], long_b[2], sent = tie((long_a[2], long_b[2], sent))
             own_came = sibling(sent)
         else:
-            long_a[k], long_b[k] = beside((long_a[k], long_b[k]), k - 2 if k <= full else full)
+            long_a[k], long_b[k] = beside((long_a[k], long_b[k]), 0 if k <= full else full)
     far = join([long_a[-1], long_b[-1]])
     far_a, far_b, sent = near(far, sibling(far), 2)
 
@@ -269,6 +269,7 @@
                 behind(part(k - 1, 1, by_short_b)),
                 ahead(part(k - 1, 2, by_short_a)),
             )
+            by_long_a, by_long_b = beside((by_long_a, by_long_b), k - 2)
     return combine(
         (half, [(own_kept, 0), (own_came, 0), (by_long_a, 0), (by_short_a, 0)]),
         (half, [(own_kept, half), (own_came, half), (by_long_b, 0), (by_short_b, 0)]),

time: 114 us -> 119 us (1.044)
  waiting for transfers between devices: 43.8 us -> 49.4 us
  starting transfers between devices: 32.2 us -> 30.8 us
    ppermute x28, waiting for transfers between devices: 41.9 us -> 48.1 us  [shift(): return lambda x: lax.ppermute(x, 'expert', pairs)]
    ppermute x28, starting transfers between devices: 30.2 us -> 28.6 us  [shift(): return lambda x: lax.ppermute(x, 'expert', pairs)]
  transfers between devices with their start and end apart: 38 -> 38, of which waited for: 20 -> 19; matrix products, arithmetic and copies ran while one was open for 0% -> 0% of each run, Pallas kernels for 25% -> 24%
where the time goes in v1:
time: 119 us; the launch traced here: 118 us
  waiting for transfers between devices  49.4 us (42%)
  Pallas kernels  32.1 us (27%)
  starting transfers between devices  30.8 us (26%)
  local copies, waits for them, and re-layouts  5.68 us (5%)
    ppermute x28, waiting for transfers between devices, shift(): return lambda x: lax.ppermute(x, 'expert', pairs)  48.1 us
    ppermute x28, starting transfers between devices, shift(): return lambda x: lax.ppermute(x, 'expert', pairs)  28.6 us
    pallas_call x5, Pallas kernels, ffn(): pl.pallas_call(functools.partial(ffn_kernel, heights, splits), out_shape=...  27 us
    unnamed x12, local copies, waits for them, and re-layouts  5.68 us
    pallas_call x1, Pallas kernels, pack(): pl.pallas_call(pack_kernel, out_shape=[jax.ShapeDtypeStruct((r, width + l...  2.62 us
  transfers between devices with their start and end apart: 38, of which 19 were waited for; matrix products, arithmetic and copies ran while one was open for 0% of the time, Pallas kernels for 24%

profile of v1, /device:TPU:0, one launch (start us, length us, event | category | flops | bytes accessed | tf_op | source)
XLA Modules:
  0.0 118.3 jit_solution(5424026080655301990)
XLA Ops:
  0.0 2.6 %pack_rows.1 = (bf16[128,2176]{1,0:T(8,128)(2,1)}, bf16[64,2176]{1,0:T(8,128)(2,1)}, bf16[64,2176]{1,0:T(8,128)(2,1)}) custom-call(bf16[128,2048]{1,0:T(8,128)(2,1)} %refs_0_.2, f32[1,2048]{1,0:T(1,128)} %bitcast.22, bf16[16,2048]{1,0:T(8,128)(2,1)} %bitcast.21, s32[8,128]{1,0:T(8,128)} %bitcast.23), custom_call_target="tpu_custom_call" | custom-call | tf_op jit(solution)/shard_map/pack_rows/pallas_call | solution.py:57
  3.2 2.6 %collective-permute-start.1 = (bf16[64,2176]{1,0:T(8,128)(2,1)}, bf16[64,2176]{1,0:T(8,128)(2,1)S(1)}, u32[]{:S(2)}, u32[]{:S(2)}) collective-permute-start(bf16[64,2176]{1,0:T(8,128)(2,1)} %get-tuple-element.46), channel_id=1, source_target_pairs={{0,4},{1,5},{4,8},{5,9},{8,12},{9,13},{12,14},{13,15},{14,10},{15,... | collective-permute-start | bytes 835592 | tf_op jit(solution)/shard_map/ppermute | solution.py:198
  5.8 1.9 %collective-permute-start.7 = (bf16[64,2176]{1,0:T(8,128)(2,1)}, bf16[64,2176]{1,0:T(8,128)(2,1)S(1)}, u32[]{:S(2)}, u32[]{:S(2)}) collective-permute-start(bf16[64,2176]{1,0:T(8,128)(2,1)} %get-tuple-element.46), channel_id=1, source_target_pairs={{0,2},{1,3},{4,0},{5,1},{8,4},{9,5},{12,8},{13,9},{14,12},{15,13},... | collective-permute-start | bytes 835592 | tf_op jit(solution)/shard_map/ppermute | solution.py:198
  7.9 1.9 %copy-done = bf16[1,2048,768]{2,1,0:T(8,128)(2,1)S(1)} copy-done((bf16[1,2048,768]{2,1,0:T(8,128)(2,1)S(1)}, bf16[1,2048,768]{2,1,0:T(8,128)(2,1)}, u32[]{:S(2)}) %copy-start) | copy-done | bytes 3145752
  9.8 1.9 %copy-done.2 = bf16[1,2048,768]{2,1,0:T(8,128)(2,1)S(1)} copy-done((bf16[1,2048,768]{2,1,0:T(8,128)(2,1)S(1)}, bf16[1,2048,768]{2,1,0:T(8,128)(2,1)}, u32[]{:S(2)}) %copy-start.2) | copy-done | bytes 3145752
  11.6 1.9 %copy-done.4 = bf16[1,768,2048]{2,1,0:T(8,128)(2,1)S(1)} copy-done((bf16[1,768,2048]{2,1,0:T(8,128)(2,1)S(1)}, bf16[1,768,2048]{2,1,0:T(8,128)(2,1)}, u32[]{:S(2)}) %copy-start.4) | copy-done | bytes 3145752
  13.6 1.9 %collective-permute-done.2.refs_3_ = bf16[64,2176]{1,0:T(8,128)(2,1)S(1)} collective-permute-done((bf16[64,2176]{1,0:T(8,128)(2,1)}, bf16[64,2176]{1,0:T(8,128)(2,1)S(1)}, u32[]{:S(2)}, u32[]{:S(2)}) %collective-permute-start.2) | collective-permute-done | bytes 278560 | tf_op jit(solution)/shard_map/ppermute | solution.py:198
  15.5 1.6 %collective-permute-start.3 = (bf16[64,2176]{1,0:T(8,128)(2,1)S(1)}, bf16[64,2176]{1,0:T(8,128)(2,1)S(1)}, u32[]{:S(2)}, u32[]{:S(2)}) collective-permute-start(bf16[64,2176]{1,0:T(8,128)(2,1)S(1)} %collective-permute-done.1.refs_0_), channel_id=1, source_target_pairs={{0,4},{1,5},{4,8},{5,9},{8,12},{9,13},{12,14},{13,15},{14,10},{15,... | collective-permute-start | bytes 835592 | tf_op jit(solution)/shard_map/ppermute | solution.py:198
  17.5 3.9 %collective-permute-done.7.refs_2_ = bf16[64,2176]{1,0:T(8,128)(2,1)S(1)} collective-permute-done((bf16[64,2176]{1,0:T(8,128)(2,1)}, bf16[64,2176]{1,0:T(8,128)(2,1)S(1)}, u32[]{:S(2)}, u32[]{:S(2)}) %collective-permute-start.7) | collective-permute-done | bytes 278560 | tf_op jit(solution)/shard_map/ppermute | solution.py:198
  21.5 2.0 %collective-permute-start.10 = (bf16[64,2176]{1,0:T(8,128)(2,1)S(1)}, bf16[64,2176]{1,0:T(8,128)(2,1)S(1)}, u32[]{:S(2)}, u32[]{:S(2)}) collective-permute-start(bf16[64,2176]{1,0:T(8,128)(2,1)S(1)} %collective-permute-done.6.refs_1_), channel_id=1, source_target_pairs={{0,4},{1,5},{4,8},{5,9},{8,12},{9,13},{12,14},{13,15},{14,10},{15,... | collective-permute-start | bytes 835592 | tf_op jit(solution)/shard_map/ppermute | solution.py:198
  23.5 3.9 %expert_ffn.5 = (bf16[128,2048]{1,0:T(8,128)(2,1)S(1)}, bf16[128,2048]{1,0:T(8,128)(2,1)S(1)}) custom-call(bf16[128,2176]{1,0:T(8,128)(2,1)S(1)} %copy-done.5, bf16[128,2176]{1,0:T(8,128)(2,1)S(1)} %collective-permute-done.refs_1_, bf16[2048,768]{1,0:T(8,128)(2,1)S(1)} %bitcast.6, bf16[2048,768]{1,0:T(8,128)(2,1)S(1)} %bitcast.11, ...), custom_call_target="tpu_custom_call" | custom-call | flops 2415919104 | bytes 524288 | tf_op jit(solution)/shard_map/expert_ffn/pallas_call | solution.py:111
  27.5 1.6 %collective-permute-start.9 = (bf16[64,2176]{1,0:T(8,128)(2,1)S(1)}, bf16[64,2176]{1,0:T(8,128)(2,1)S(1)}, u32[]{:S(2)}, u32[]{:S(2)}) collective-permute-start(bf16[64,2176]{1,0:T(8,128)(2,1)S(1)} %collective-permute-done.3.refs_0_), channel_id=1, source_target_pairs={{0,4},{1,5},{4,8},{5,9},{8,12},{9,13},{12,14},{13,15},{14,10},{15,... | collective-permute-start | bytes 835592 | tf_op jit(solution)/shard_map/ppermute | solution.py:198
  29.1 3.6 %collective-permute-done.12.refs_2_ = bf16[64,2176]{1,0:T(8,128)(2,1)S(1)} collective-permute-done((bf16[64,2176]{1,0:T(8,128)(2,1)S(1)}, bf16[64,2176]{1,0:T(8,128)(2,1)S(1)}, u32[]{:S(2)}, u32[]{:S(2)}) %collective-permute-start.12) | collective-permute-done | bytes 278560 | tf_op jit(solution)/shard_map/ppermute | solution.py:198
  32.9 1.7 %collective-permute-start.11 = (bf16[64,2176]{1,0:T(8,128)(2,1)S(1)}, bf16[64,2176]{1,0:T(8,128)(2,1)S(1)}, u32[]{:S(2)}, u32[]{:S(2)}) collective-permute-start(bf16[64,2176]{1,0:T(8,128)(2,1)S(1)} %collective-permute-done.10.refs_1_), channel_id=1, source_target_pairs={{0,4},{1,5},{4,8},{5,9},{8,12},{9,13},{12,14},{13,15},{14,10},{15,... | collective-permute-start | bytes 835592 | tf_op jit(solution)/shard_map/ppermute | solution.py:198
  34.9 7.3 %collective-permute-done.13.refs_2_ = bf16[64,2176]{1,0:T(8,128)(2,1)S(1)} collective-permute-done((bf16[64,2176]{1,0:T(8,128)(2,1)S(1)}, bf16[64,2176]{1,0:T(8,128)(2,1)S(1)}, u32[]{:S(2)}, u32[]{:S(2)}) %collective-permute-start.13) | collective-permute-done | bytes 278560 | tf_op jit(solution)/shard_map/ppermute | solution.py:198
  43.1 3.4 %collective-permute-done.14.refs_3_ = bf16[64,2176]{1,0:T(8,128)(2,1)S(1)} collective-permute-done((bf16[64,2176]{1,0:T(8,128)(2,1)S(1)}, bf16[64,2176]{1,0:T(8,128)(2,1)S(1)}, u32[]{:S(2)}, u32[]{:S(2)}) %collective-permute-start.14) | collective-permute-done | bytes 278560 | tf_op jit(solution)/shard_map/ppermute | solution.py:198
  46.7 1.6 %collective-permute-start.16 = (bf16[64,2176]{1,0:T(8,128)(2,1)S(1)}, bf16[64,2176]{1,0:T(8,128)(2,1)S(1)}, u32[]{:S(2)}, u32[]{:S(2)}) collective-permute-start(bf16[64,2176]{1,0:T(8,128)(2,1)S(1)} %collective-permute-done.9.refs_0_), channel_id=1, source_target_pairs={{0,4},{1,5},{4,8},{5,9},{8,12},{9,13},{12,14},{13,15},{14,10},{15,... | collective-permute-start | bytes 835592 | tf_op jit(solution)/shard_map/ppermute | solution.py:198
  49.4 6.4 %expert_ffn.7 = (bf16[64,2048]{1,0:T(8,128)(2,1)S(1)}, bf16[64,2048]{1,0:T(8,128)(2,1)S(1)}, bf16[64,2048]{1,0:T(8,128)(2,1)S(1)}, bf16[64,2048]{1,0:T(8,128)(2,1)S(1)}, bf16[256,2048]{1,0:T(8,128)(2,1)S(1)}) custom-call(bf16[256,2176]{1,0:T(8,128)(2,1)S(1)} %join_rows.5.refs_0_, bf16[256,2176]{1,0:T(8,128)(2,1)S(1)} %collective-permute-done.15.refs_1_, ...), custom_call_target="tpu_custom_call" | custom-call | flops 4831838208 | bytes 1048576 | tf_op jit(solution)/shard_map/expert_ffn/pallas_call | solution.py:111
  59.1 3.9 %expert_ffn.8 = (bf16[64,2048]{1,0:T(8,128)(2,1)S(1)}, bf16[64,2048]{1,0:T(8,128)(2,1)S(1)}, bf16[128,2048]{1,0:T(8,128)(2,1)S(1)}) custom-call(bf16[128,2176]{1,0:T(8,128)(2,1)S(1)} %join_rows.6.refs_0_, bf16[128,2176]{1,0:T(8,128)(2,1)S(1)} %collective-permute-done.19.refs_1_, bf16[2048,768]{1,0:T(8,128)(2,1)S(1)} %bitcast.8, ...), custom_call_target="tpu_custom_call" | custom-call | flops 2415919104 | bytes 524288 | tf_op jit(solution)/shard_map/expert_ffn/pallas_call | solution.py:111
  63.3 1.6 %collective-permute-start.23 = (bf16[64,2048]{1,0:T(8,128)(2,1)S(1)}, bf16[64,2048]{1,0:T(8,128)(2,1)S(1)}, u32[]{:S(2)}, u32[]{:S(2)}) collective-permute-start(bf16[64,2048]{1,0:T(8,128)(2,1)S(1)} %combine_rows.17), channel_id=1, source_target_pairs={{0,4},{1,5},{4,8},{5,9},{8,12},{9,13},{12,14},{13,15},{14,10},{15,... | collective-permute-start | bytes 786440 | tf_op jit(solution)/shard_map/ppermute | solution.py:198
  66.1 1.6 %collective-permute-start.22 = (bf16[64,2048]{1,0:T(8,128)(2,1)S(1)}, bf16[64,2048]{1,0:T(8,128)(2,1)S(1)}, u32[]{:S(2)}, u32[]{:S(2)}) collective-permute-start(bf16[64,2048]{1,0:T(8,128)(2,1)S(1)} %combine_rows.16), channel_id=1, source_target_pairs={{0,4},{1,5},{4,8},{5,9},{8,12},{9,13},{12,14},{13,15},{14,10},{15,... | collective-permute-start | bytes 786440 | tf_op jit(solution)/shard_map/ppermute | solution.py:198
  67.8 6.4 %expert_ffn.9 = (bf16[64,2048]{1,0:T(8,128)(2,1)S(1)}, bf16[64,2048]{1,0:T(8,128)(2,1)S(1)}, bf16[64,2048]{1,0:T(8,128)(2,1)S(1)}, bf16[64,2048]{1,0:T(8,128)(2,1)S(1)}, bf16[256,2048]{1,0:T(8,128)(2,1)S(1)}) custom-call(bf16[256,2176]{1,0:T(8,128)(2,1)S(1)} %join_rows.7.refs_0_, bf16[256,2176]{1,0:T(8,128)(2,1)S(1)} %collective-permute-done.25.refs_1_, ...), custom_call_target="tpu_custom_call" | custom-call | flops 4831838208 | bytes 1048576 | tf_op jit(solution)/shard_map/expert_ffn/pallas_call | solution.py:111
  74.2 4.7 %collective-permute-done.21.refs_2_ = bf16[64,2048]{1,0:T(8,128)(2,1)S(1)} collective-permute-done((bf16[64,2048]{1,0:T(8,128)(2,1)S(1)}, bf16[64,2048]{1,0:T(8,128)(2,1)S(1)}, u32[]{:S(2)}, u32[]{:S(2)}) %collective-permute-start.21) | collective-permute-done | bytes 262176 | tf_op jit(solution)/shard_map/ppermute | solution.py:198
  79.0 1.5 %collective-permute-start.27 = (bf16[64,2048]{1,0:T(8,128)(2,1)S(1)}, bf16[64,2048]{1,0:T(8,128)(2,1)S(1)}, u32[]{:S(2)}, u32[]{:S(2)}) collective-permute-start(bf16[64,2048]{1,0:T(8,128)(2,1)S(1)} %combine_rows.20), channel_id=1, source_target_pairs={{0,4},{1,5},{4,8},{5,9},{8,12},{9,13},{12,14},{13,15},{14,10},{15,... | collective-permute-start | bytes 786440 | tf_op jit(solution)/shard_map/ppermute | solution.py:198
  81.3 6.4 %expert_ffn.6 = (bf16[64,2048]{1,0:T(8,128)(2,1)S(1)}, bf16[64,2048]{1,0:T(8,128)(2,1)S(1)}, bf16[64,2048]{1,0:T(8,128)(2,1)S(1)}, bf16[64,2048]{1,0:T(8,128)(2,1)S(1)}, bf16[256,2048]{1,0:T(8,128)(2,1)S(1)}) custom-call(bf16[256,2176]{1,0:T(8,128)(2,1)S(1)} %join_rows.4.refs_0_, bf16[256,2176]{1,0:T(8,128)(2,1)S(1)} %collective-permute-done.8.refs_1_, ...), custom_call_target="tpu_custom_call" | custom-call | flops 4831838208 | bytes 1048576 | tf_op jit(solution)/shard_map/expert_ffn/pallas_call | solution.py:111
  90.2 1.5 %collective-permute-start.32 = (bf16[64,2048]{1,0:T(8,128)(2,1)S(1)}, bf16[64,2048]{1,0:T(8,128)(2,1)S(1)}, u32[]{:S(2)}, u32[]{:S(2)}) collective-permute-start(bf16[64,2048]{1,0:T(8,128)(2,1)S(1)} %combine_rows.23), channel_id=1, source_target_pairs={{0,4},{1,5},{4,8},{5,9},{8,12},{9,13},{12,14},{13,15},{14,10},{15,... | collective-permute-start | bytes 786440 | tf_op jit(solution)/shard_map/ppermute | solution.py:198
  92.5 5.6 %collective-permute-done.30.refs_2_ = bf16[64,2048]{1,0:T(8,128)(2,1)S(1)} collective-permute-done((bf16[64,2048]{1,0:T(8,128)(2,1)S(1)}, bf16[64,2048]{1,0:T(8,128)(2,1)S(1)}, u32[]{:S(2)}, u32[]{:S(2)}) %collective-permute-start.30) | collective-permute-done | bytes 262176 | tf_op jit(solution)/shard_map/ppermute | solution.py:198
  99.5 1.5 %collective-permute-start.33 = (bf16[64,2048]{1,0:T(8,128)(2,1)S(1)}, bf16[64,2048]{1,0:T(8,128)(2,1)S(1)}, u32[]{:S(2)}, u32[]{:S(2)}) collective-permute-start(bf16[64,2048]{1,0:T(8,128)(2,1)S(1)} %combine_rows.24), channel_id=1, source_target_pairs={{0,4},{1,5},{4,8},{5,9},{8,12},{9,13},{12,14},{13,15},{14,10},{15,... | collective-permute-start | bytes 786440 | tf_op jit(solution)/shard_map/ppermute | solution.py:198
  101.0 4.0 %collective-permute-done.34.refs_2_ = bf16[64,2048]{1,0:T(8,128)(2,1)S(1)} collective-permute-done((bf16[64,2048]{1,0:T(8,128)(2,1)S(1)}, bf16[64,2048]{1,0:T(8,128)(2,1)S(1)}, u32[]{:S(2)}, u32[]{:S(2)}) %collective-permute-start.34) | collective-permute-done | bytes 262176 | tf_op jit(solution)/shard_map/ppermute | solution.py:198
  107.9 4.9 %collective-permute-done.31.refs_2_ = bf16[64,2048]{1,0:T(8,128)(2,1)S(1)} collective-permute-done((bf16[64,2048]{1,0:T(8,128)(2,1)S(1)}, bf16[64,2048]{1,0:T(8,128)(2,1)S(1)}, u32[]{:S(2)}, u32[]{:S(2)}) %collective-permute-start.31) | collective-permute-done | bytes 262176 | tf_op jit(solution)/shard_map/ppermute | solution.py:198
  112.9 2.7 %collective-permute-done.35.refs_6_ = bf16[64,2048]{1,0:T(8,128)(2,1)S(1)} collective-permute-done((bf16[64,2048]{1,0:T(8,128)(2,1)S(1)}, bf16[64,2048]{1,0:T(8,128)(2,1)S(1)}, u32[]{:S(2)}, u32[]{:S(2)}) %collective-permute-start.35) | collective-permute-done | bytes 262176 | tf_op jit(solution)/shard_map/ppermute | solution.py:198
  115.6 1.6 %collective-permute-done.37.refs_7_ = bf16[64,2048]{1,0:T(8,128)(2,1)S(1)} collective-permute-done((bf16[64,2048]{1,0:T(8,128)(2,1)S(1)}, bf16[64,2048]{1,0:T(8,128)(2,1)S(1)}, u32[]{:S(2)}, u32[]{:S(2)}) %collective-permute-start.37) | collective-permute-done | bytes 262176 | tf_op jit(solution)/shard_map/ppermute | solution.py:198
  (83 shorter events, 18.0 us)
Async XLA Ops:
  2.6 20.9 %collective-permute-start = (bf16[128,2176]{1,0:T(8,128)(2,1)}, bf16[128,2176]{1,0:T(8,128)(2,1)S(1)}, u32[]{:S(2)}, u32[]{:S(2)}) collective-permute-start(bf16[128,2176]{1,0:T(8,128)(2,1)} %get-tuple-element.45.refs_0_), channel_id=1, source_target_pairs={{0,1},{1,0},{2,3},{3,2},{4,5},{5,4},{6,7},{7,6},{8,9},{9,8},{10,11... | collective-permute-start | bytes 1671176 | tf_op jit(solution)/shard_map/ppermute | solution.py:203
  3.2 10.4 %collective-permute-start.1 = (bf16[64,2176]{1,0:T(8,128)(2,1)}, bf16[64,2176]{1,0:T(8,128)(2,1)S(1)}, u32[]{:S(2)}, u32[]{:S(2)}) collective-permute-start(bf16[64,2176]{1,0:T(8,128)(2,1)} %get-tuple-element.46), channel_id=1, source_target_pairs={{0,4},{1,5},{4,8},{5,9},{8,12},{9,13},{12,14},{13,15},{14,10},{15,... | collective-permute-start | bytes 835592 | tf_op jit(solution)/shard_map/ppermute | solution.py:198
  5.8 9.7 %collective-permute-start.2 = (bf16[64,2176]{1,0:T(8,128)(2,1)}, bf16[64,2176]{1,0:T(8,128)(2,1)S(1)}, u32[]{:S(2)}, u32[]{:S(2)}) collective-permute-start(bf16[64,2176]{1,0:T(8,128)(2,1)} %get-tuple-element.47), channel_id=1, source_target_pairs={{0,2},{1,3},{4,0},{5,1},{8,4},{9,5},{12,8},{13,9},{14,12},{15,13},... | collective-permute-start | bytes 835592 | tf_op jit(solution)/shard_map/ppermute | solution.py:198
  5.8 15.7 %collective-permute-start.7 = (bf16[64,2176]{1,0:T(8,128)(2,1)}, bf16[64,2176]{1,0:T(8,128)(2,1)S(1)}, u32[]{:S(2)}, u32[]{:S(2)}) collective-permute-start(bf16[64,2176]{1,0:T(8,128)(2,1)} %get-tuple-element.46), channel_id=1, source_target_pairs={{0,2},{1,3},{4,0},{5,1},{8,4},{9,5},{12,8},{13,9},{14,12},{15,13},... | collective-permute-start | bytes 835592 | tf_op jit(solution)/shard_map/ppermute | solution.py:198
  7.8 13.7 %collective-permute-start.6 = (bf16[64,2176]{1,0:T(8,128)(2,1)}, bf16[64,2176]{1,0:T(8,128)(2,1)S(1)}, u32[]{:S(2)}, u32[]{:S(2)}) collective-permute-start(bf16[64,2176]{1,0:T(8,128)(2,1)} %get-tuple-element.47), channel_id=1, source_target_pairs={{0,4},{1,5},{4,8},{5,9},{8,12},{9,13},{12,14},{13,15},{14,10},{15,... | collective-permute-start | bytes 835592 | tf_op jit(solution)/shard_map/ppermute | solution.py:198
  15.5 11.9 %collective-permute-start.3 = (bf16[64,2176]{1,0:T(8,128)(2,1)S(1)}, bf16[64,2176]{1,0:T(8,128)(2,1)S(1)}, u32[]{:S(2)}, u32[]{:S(2)}) collective-permute-start(bf16[64,2176]{1,0:T(8,128)(2,1)S(1)} %collective-permute-done.1.refs_0_), channel_id=1, source_target_pairs={{0,4},{1,5},{4,8},{5,9},{8,12},{9,13},{12,14},{13,15},{14,10},{15,... | collective-permute-start | bytes 835592 | tf_op jit(solution)/shard_map/ppermute | solution.py:198
  17.1 10.4 %collective-permute-start.4 = (bf16[64,2176]{1,0:T(8,128)(2,1)S(1)}, bf16[64,2176]{1,0:T(8,128)(2,1)S(1)}, u32[]{:S(2)}, u32[]{:S(2)}) collective-permute-start(bf16[64,2176]{1,0:T(8,128)(2,1)S(1)} %collective-permute-done.2.refs_3_), channel_id=1, source_target_pairs={{0,2},{1,3},{4,0},{5,1},{8,4},{9,5},{12,8},{13,9},{14,12},{15,13},... | collective-permute-start | bytes 835592 | tf_op jit(solution)/shard_map/ppermute | solution.py:198
  21.5 11.2 %collective-permute-start.12 = (bf16[64,2176]{1,0:T(8,128)(2,1)S(1)}, bf16[64,2176]{1,0:T(8,128)(2,1)S(1)}, u32[]{:S(2)}, u32[]{:S(2)}) collective-permute-start(bf16[64,2176]{1,0:T(8,128)(2,1)S(1)} %collective-permute-done.7.refs_2_), channel_id=1, source_target_pairs={{0,2},{1,3},{4,0},{5,1},{8,4},{9,5},{12,8},{13,9},{14,12},{15,13},... | collective-permute-start | bytes 835592 | tf_op jit(solution)/shard_map/ppermute | solution.py:198
  21.5 11.4 %collective-permute-start.10 = (bf16[64,2176]{1,0:T(8,128)(2,1)S(1)}, bf16[64,2176]{1,0:T(8,128)(2,1)S(1)}, u32[]{:S(2)}, u32[]{:S(2)}) collective-permute-start(bf16[64,2176]{1,0:T(8,128)(2,1)S(1)} %collective-permute-done.6.refs_1_), channel_id=1, source_target_pairs={{0,4},{1,5},{4,8},{5,9},{8,12},{9,13},{12,14},{13,15},{14,10},{15,... | collective-permute-start | bytes 835592 | tf_op jit(solution)/shard_map/ppermute | solution.py:198
  27.5 15.6 %collective-permute-start.9 = (bf16[64,2176]{1,0:T(8,128)(2,1)S(1)}, bf16[64,2176]{1,0:T(8,128)(2,1)S(1)}, u32[]{:S(2)}, u32[]{:S(2)}) collective-permute-start(bf16[64,2176]{1,0:T(8,128)(2,1)S(1)} %collective-permute-done.3.refs_0_), channel_id=1, source_target_pairs={{0,4},{1,5},{4,8},{5,9},{8,12},{9,13},{12,14},{13,15},{14,10},{15,... | collective-permute-start | bytes 835592 | tf_op jit(solution)/shard_map/ppermute | solution.py:198
  32.6 9.6 %collective-permute-start.13 = (bf16[64,2176]{1,0:T(8,128)(2,1)S(1)}, bf16[64,2176]{1,0:T(8,128)(2,1)S(1)}, u32[]{:S(2)}, u32[]{:S(2)}) collective-permute-start(bf16[64,2176]{1,0:T(8,128)(2,1)S(1)} %collective-permute-done.12.refs_2_), channel_id=1, source_target_pairs={{0,2},{1,3},{4,0},{5,1},{8,4},{9,5},{12,8},{13,9},{14,12},{15,13},... | collective-permute-start | bytes 835592 | tf_op jit(solution)/shard_map/ppermute | solution.py:198
  32.9 10.1 %collective-permute-start.11 = (bf16[64,2176]{1,0:T(8,128)(2,1)S(1)}, bf16[64,2176]{1,0:T(8,128)(2,1)S(1)}, u32[]{:S(2)}, u32[]{:S(2)}) collective-permute-start(bf16[64,2176]{1,0:T(8,128)(2,1)S(1)} %collective-permute-done.10.refs_1_), channel_id=1, source_target_pairs={{0,4},{1,5},{4,8},{5,9},{8,12},{9,13},{12,14},{13,15},{14,10},{15,... | collective-permute-start | bytes 835592 | tf_op jit(solution)/shard_map/ppermute | solution.py:198
  34.7 11.8 %collective-permute-start.14 = (bf16[64,2176]{1,0:T(8,128)(2,1)S(1)}, bf16[64,2176]{1,0:T(8,128)(2,1)S(1)}, u32[]{:S(2)}, u32[]{:S(2)}) collective-permute-start(bf16[64,2176]{1,0:T(8,128)(2,1)S(1)} %collective-permute-done.4.refs_3_), channel_id=1, source_target_pairs={{0,2},{1,3},{4,0},{5,1},{8,4},{9,5},{12,8},{13,9},{14,12},{15,13},... | collective-permute-start | bytes 835592 | tf_op jit(solution)/shard_map/ppermute | solution.py:198
  46.7 9.1 %collective-permute-start.16 = (bf16[64,2176]{1,0:T(8,128)(2,1)S(1)}, bf16[64,2176]{1,0:T(8,128)(2,1)S(1)}, u32[]{:S(2)}, u32[]{:S(2)}) collective-permute-start(bf16[64,2176]{1,0:T(8,128)(2,1)S(1)} %collective-permute-done.9.refs_0_), channel_id=1, source_target_pairs={{0,4},{1,5},{4,8},{5,9},{8,12},{9,13},{12,14},{13,15},{14,10},{15,... | collective-permute-start | bytes 835592 | tf_op jit(solution)/shard_map/ppermute | solution.py:198
  57.2 8.9 %collective-permute-start.25 = (bf16[256,2176]{1,0:T(8,128)(2,1)S(1)}, bf16[256,2176]{1,0:T(8,128)(2,1)S(1)}, u32[]{:S(2)}, u32[]{:S(2)}) collective-permute-start(bf16[256,2176]{1,0:T(8,128)(2,1)S(1)} %join_rows.7.refs_0_), channel_id=1, source_target_pairs={{0,1},{1,0},{2,3},{3,2},{4,5},{5,4},{6,7},{7,6},{8,9},{9,8},{10,11... | collective-permute-start | bytes 3342344 | tf_op jit(solution)/shard_map/ppermute | solution.py:203
  57.9 23.3 %collective-permute-start.8 = (bf16[256,2176]{1,0:T(8,128)(2,1)S(1)}, bf16[256,2176]{1,0:T(8,128)(2,1)S(1)}, u32[]{:S(2)}, u32[]{:S(2)}) collective-permute-start(bf16[256,2176]{1,0:T(8,128)(2,1)S(1)} %join_rows.4.refs_0_), channel_id=1, source_target_pairs={{0,1},{1,0},{2,3},{3,2},{4,5},{5,4},{6,7},{7,6},{8,9},{9,8},{10,11... | collective-permute-start | bytes 3342344 | tf_op jit(solution)/shard_map/ppermute | solution.py:203
  63.3 10.9 %collective-permute-start.23 = (bf16[64,2048]{1,0:T(8,128)(2,1)S(1)}, bf16[64,2048]{1,0:T(8,128)(2,1)S(1)}, u32[]{:S(2)}, u32[]{:S(2)}) collective-permute-start(bf16[64,2048]{1,0:T(8,128)(2,1)S(1)} %combine_rows.17), channel_id=1, source_target_pairs={{0,4},{1,5},{4,8},{5,9},{8,12},{9,13},{12,14},{13,15},{14,10},{15,... | collective-permute-start | bytes 786440 | tf_op jit(solution)/shard_map/ppermute | solution.py:198
  65.0 9.2 %collective-permute-start.24 = (bf16[64,2048]{1,0:T(8,128)(2,1)S(1)}, bf16[64,2048]{1,0:T(8,128)(2,1)S(1)}, u32[]{:S(2)}, u32[]{:S(2)}) collective-permute-start(bf16[64,2048]{1,0:T(8,128)(2,1)S(1)} %combine_rows.18), channel_id=1, source_target_pairs={{0,2},{1,3},{4,0},{5,1},{8,4},{9,5},{12,8},{13,9},{14,12},{15,13},... | collective-permute-start | bytes 786440 | tf_op jit(solution)/shard_map/ppermute | solution.py:198
  65.6 13.4 %collective-permute-start.21 = (bf16[64,2048]{1,0:T(8,128)(2,1)S(1)}, bf16[64,2048]{1,0:T(8,128)(2,1)S(1)}, u32[]{:S(2)}, u32[]{:S(2)}) collective-permute-start(bf16[64,2048]{1,0:T(8,128)(2,1)S(1)} %combine_rows.15), channel_id=1, source_target_pairs={{0,2},{1,3},{4,0},{5,1},{8,4},{9,5},{12,8},{13,9},{14,12},{15,13},... | collective-permute-start | bytes 786440 | tf_op jit(solution)/shard_map/ppermute | solution.py:198
  66.1 12.8 %collective-permute-start.22 = (bf16[64,2048]{1,0:T(8,128)(2,1)S(1)}, bf16[64,2048]{1,0:T(8,128)(2,1)S(1)}, u32[]{:S(2)}, u32[]{:S(2)}) collective-permute-start(bf16[64,2048]{1,0:T(8,128)(2,1)S(1)} %combine_rows.16), channel_id=1, source_target_pairs={{0,4},{1,5},{4,8},{5,9},{8,12},{9,13},{12,14},{13,15},{14,10},{15,... | collective-permute-start | bytes 786440 | tf_op jit(solution)/shard_map/ppermute | solution.py:198
  78.9 10.2 %collective-permute-start.29 = (bf16[256,2048]{1,0:T(8,128)(2,1)S(1)}, bf16[256,2048]{1,0:T(8,128)(2,1)S(1)}, u32[]{:S(2)}, u32[]{:S(2)}) collective-permute-start(bf16[256,2048]{1,0:T(8,128)(2,1)S(1)} %get-tuple-element.74), channel_id=1, source_target_pairs={{0,1},{1,0},{2,3},{3,2},{4,5},{5,4},{6,7},{7,6},{8,9},{9,8},{10,11... | collective-permute-start | bytes 3145736 | tf_op jit(solution)/shard_map/ppermute | solution.py:203
  79.0 8.8 %collective-permute-start.27 = (bf16[64,2048]{1,0:T(8,128)(2,1)S(1)}, bf16[64,2048]{1,0:T(8,128)(2,1)S(1)}, u32[]{:S(2)}, u32[]{:S(2)}) collective-permute-start(bf16[64,2048]{1,0:T(8,128)(2,1)S(1)} %combine_rows.20), channel_id=1, source_target_pairs={{0,4},{1,5},{4,8},{5,9},{8,12},{9,13},{12,14},{13,15},{14,10},{15,... | collective-permute-start | bytes 786440 | tf_op jit(solution)/shard_map/ppermute | solution.py:198
  89.2 9.4 %collective-permute-start.28 = (bf16[256,2048]{1,0:T(8,128)(2,1)S(1)}, bf16[256,2048]{1,0:T(8,128)(2,1)S(1)}, u32[]{:S(2)}, u32[]{:S(2)}) collective-permute-start(bf16[256,2048]{1,0:T(8,128)(2,1)S(1)} %get-tuple-element.72), channel_id=1, source_target_pairs={{0,1},{1,0},{2,3},{3,2},{4,5},{5,4},{6,7},{7,6},{8,9},{9,8},{10,11... | collective-permute-start | bytes 3145736 | tf_op jit(solution)/shard_map/ppermute | solution.py:203
  89.3 8.8 %collective-permute-start.30 = (bf16[64,2048]{1,0:T(8,128)(2,1)S(1)}, bf16[64,2048]{1,0:T(8,128)(2,1)S(1)}, u32[]{:S(2)}, u32[]{:S(2)}) collective-permute-start(bf16[64,2048]{1,0:T(8,128)(2,1)S(1)} %combine_rows.21), channel_id=1, source_target_pairs={{0,2},{1,3},{4,0},{5,1},{8,4},{9,5},{12,8},{13,9},{14,12},{15,13},... | collective-permute-start | bytes 786440 | tf_op jit(solution)/shard_map/ppermute | solution.py:198
  89.9 18.1 %collective-permute-start.5 = (bf16[128,2048]{1,0:T(8,128)(2,1)S(1)}, bf16[128,2048]{1,0:T(8,128)(2,1)S(1)}, u32[]{:S(2)}, u32[]{:S(2)}) collective-permute-start(bf16[128,2048]{1,0:T(8,128)(2,1)S(1)} %get-tuple-element.53), channel_id=1, source_target_pairs={{0,1},{1,0},{2,3},{3,2},{4,5},{5,4},{6,7},{7,6},{8,9},{9,8},{10,11... | collective-permute-start | bytes 1572872 | tf_op jit(solution)/shard_map/ppermute | solution.py:203
  90.2 9.2 %collective-permute-start.32 = (bf16[64,2048]{1,0:T(8,128)(2,1)S(1)}, bf16[64,2048]{1,0:T(8,128)(2,1)S(1)}, u32[]{:S(2)}, u32[]{:S(2)}) collective-permute-start(bf16[64,2048]{1,0:T(8,128)(2,1)S(1)} %combine_rows.23), channel_id=1, source_target_pairs={{0,4},{1,5},{4,8},{5,9},{8,12},{9,13},{12,14},{13,15},{14,10},{15,... | collective-permute-start | bytes 786440 | tf_op jit(solution)/shard_map/ppermute | solution.py:198
  91.8 13.2 %collective-permute-start.34 = (bf16[64,2048]{1,0:T(8,128)(2,1)S(1)}, bf16[64,2048]{1,0:T(8,128)(2,1)S(1)}, u32[]{:S(2)}, u32[]{:S(2)}) collective-permute-start(bf16[64,2048]{1,0:T(8,128)(2,1)S(1)} %combine_rows.25), channel_id=1, source_target_pairs={{0,4},{1,5},{4,8},{5,9},{8,12},{9,13},{12,14},{13,15},{14,10},{15,... | collective-permute-start | bytes 786440 | tf_op jit(solution)/shard_map/ppermute | solution.py:198
  98.0 9.2 %collective-permute-start.36 = (bf16[64,2048]{1,0:T(8,128)(2,1)S(1)}, bf16[64,2048]{1,0:T(8,128)(2,1)S(1)}, u32[]{:S(2)}, u32[]{:S(2)}) collective-permute-start(bf16[64,2048]{1,0:T(8,128)(2,1)S(1)} %combine_rows.27), channel_id=1, source_target_pairs={{0,2},{1,3},{4,0},{5,1},{8,4},{9,5},{12,8},{13,9},{14,12},{15,13},... | collective-permute-start | bytes 786440 | tf_op jit(solution)/shard_map/ppermute | solution.py:198
  98.7 14.2 %collective-permute-start.31 = (bf16[64,2048]{1,0:T(8,128)(2,1)S(1)}, bf16[64,2048]{1,0:T(8,128)(2,1)S(1)}, u32[]{:S(2)}, u32[]{:S(2)}) collective-permute-start(bf16[64,2048]{1,0:T(8,128)(2,1)S(1)} %combine_rows.22), channel_id=1, source_target_pairs={{0,2},{1,3},{4,0},{5,1},{8,4},{9,5},{12,8},{13,9},{14,12},{15,13},... | collective-permute-start | bytes 786440 | tf_op jit(solution)/shard_map/ppermute | solution.py:198
  99.5 13.4 %collective-permute-start.33 = (bf16[64,2048]{1,0:T(8,128)(2,1)S(1)}, bf16[64,2048]{1,0:T(8,128)(2,1)S(1)}, u32[]{:S(2)}, u32[]{:S(2)}) collective-permute-start(bf16[64,2048]{1,0:T(8,128)(2,1)S(1)} %combine_rows.24), channel_id=1, source_target_pairs={{0,4},{1,5},{4,8},{5,9},{8,12},{9,13},{12,14},{13,15},{14,10},{15,... | collective-permute-start | bytes 786440 | tf_op jit(solution)/shard_map/ppermute | solution.py:198
  105.1 10.5 %collective-permute-start.35 = (bf16[64,2048]{1,0:T(8,128)(2,1)S(1)}, bf16[64,2048]{1,0:T(8,128)(2,1)S(1)}, u32[]{:S(2)}, u32[]{:S(2)}) collective-permute-start(bf16[64,2048]{1,0:T(8,128)(2,1)S(1)} %combine_rows.26), channel_id=1, source_target_pairs={{0,4},{1,5},{4,8},{5,9},{8,12},{9,13},{12,14},{13,15},{14,10},{15,... | collective-permute-start | bytes 786440 | tf_op jit(solution)/shard_map/ppermute | solution.py:198
  107.4 9.9 %collective-permute-start.37 = (bf16[64,2048]{1,0:T(8,128)(2,1)S(1)}, bf16[64,2048]{1,0:T(8,128)(2,1)S(1)}, u32[]{:S(2)}, u32[]{:S(2)}) collective-permute-start(bf16[64,2048]{1,0:T(8,128)(2,1)S(1)} %combine_rows.28), channel_id=1, source_target_pairs={{0,2},{1,3},{4,0},{5,1},{8,4},{9,5},{12,8},{13,9},{14,12},{15,13},... | collective-permute-start | bytes 786440 | tf_op jit(solution)/shard_map/ppermute | solution.py:198
  (12 other events, 65.6 us)

commit v2 on v1

--- a/solution.py
+++ b/solution.py
@@ -118,7 +118,7 @@
         ],
         compiler_params=pltpu.CompilerParams(vmem_limit_bytes=20 * MIB),
         cost_estimate=pl.CostEstimate(
-            flops=6 * rows * width * depth,
+            flops=2 * rows * width * depth,
             bytes_accessed=rows * width,
             transcendentals=0,
         ),
@@ -226,13 +226,20 @@
     long_a, long_b, short_a, short_b = [first], [second], [first], [second]
     terms, came = [None] * (full + 1), [None] * (full + 1)
 
-    def beside(hops, k):
-        if k < 1:
-            return hops
-        ours = join([long_a[k], short_b[k], short_a[k], long_b[k]])
-        *terms[k], sent = near(ours, sibling(ours), 4)
-        *hops, sent = tie((*hops, sent))
-        came[k] = sibling(sent)
+    def beside(hops, *distances):
+        distances = [k for k in distances if k >= 1]
+        sents = []
+        for k in distances:
+            ours = join([long_a[k], short_b[k], short_a[k], long_b[k]])
+            theirs = sibling(ours)
+            if sents:
+                ours, theirs, sents[-1] = tie((ours, theirs, sents[-1]))
+            *terms[k], sent = near(ours, theirs, 4)
+            sents.append(sent)
+        if distances:
+            hops, sents = tie((list(hops), sents))
+        for k, sent in zip(distances, sents):
+            came[k] = sibling(sent)
         return hops
 
     for k in range(1, full + 2):
@@ -260,7 +267,7 @@
     by_long_a = behind(combine((half, [(far_a, 0), (far_came, 0)])))
     by_long_b = ahead(combine((half, [(far_b, 0), (far_came, half)])))
     by_long_a, by_long_b, by_short_a, by_short_b = beside(
-        (by_long_a, by_long_b, by_short_a, by_short_b), full - 1
+        (by_long_a, by_long_b, by_short_a, by_short_b), full - 1, full - 2
     )
     for k in range(full, 0, -1):
         by_long_a, by_long_b = behind(part(k, 0, by_long_a)), ahead(part(k, 3, by_long_b))
@@ -269,7 +276,7 @@
                 behind(part(k - 1, 1, by_short_b)),
                 ahead(part(k - 1, 2, by_short_a)),
             )
-            by_long_a, by_long_b = beside((by_long_a, by_long_b), k - 2)
+            by_long_a, by_long_b = beside((by_long_a, by_long_b), k - 3)
     return combine(
         (half, [(own_kept, 0), (own_came, 0), (by_long_a, 0), (by_short_a, 0)]),
         (half, [(own_kept, half), (own_came, half), (by_long_b, 0), (by_short_b, 0)]),

time: 119 us -> 116 us (0.975)
  waiting for transfers between devices: 49.4 us -> 45.1 us
  starting transfers between devices: 30.8 us -> 32.3 us
    ppermute x28, waiting for transfers between devices: 48.1 us -> 43.7 us  [shift(): return lambda x: lax.ppermute(x, 'expert', pairs)]
  transfers between devices with their start and end apart: 38 -> 38, of which waited for: 19 -> 15; matrix products, arithmetic and copies ran while one was open for 0% -> 0% of each run, Pallas kernels for 24% -> 25%
where the time goes in v2:
time: 116 us; the launch traced here: 115 us
  waiting for transfers between devices  45.1 us (39%)
  starting transfers between devices  32.3 us (28%)
  Pallas kernels  32.1 us (28%)
  local copies, waits for them, and re-layouts  5.68 us (5%)
    ppermute x28, waiting for transfers between devices, shift(): return lambda x: lax.ppermute(x, 'expert', pairs)  43.7 us
    ppermute x28, starting transfers between devices, shift(): return lambda x: lax.ppermute(x, 'expert', pairs)  29.7 us
    pallas_call x5, Pallas kernels, ffn(): pl.pallas_call(functools.partial(ffn_kernel, heights, splits), out_shape=...  27 us
    unnamed x12, local copies, waits for them, and re-layouts  5.68 us
    pallas_call x1, Pallas kernels, pack(): pl.pallas_call(pack_kernel, out_shape=[jax.ShapeDtypeStruct((r, width + l...  2.62 us
    ppermute x10, starting transfers between devices, sibling(): return lax.ppermute(x, 'expert', [(d, d ^ 1) for d in range(2 * chips)])  2.57 us
  transfers between devices with their start and end apart: 38, of which 15 were waited for; matrix products, arithmetic and copies ran while one was open for 0% of the time, Pallas kernels for 25%

profile of v2, /device:TPU:0, one launch (start us, length us, event | category | flops | bytes accessed | tf_op | source)
XLA Modules:
  0.0 115.4 jit_solution(1002455117821286444)
XLA Ops:
  0.0 2.6 %pack_rows.1 = (bf16[128,2176]{1,0:T(8,128)(2,1)}, bf16[64,2176]{1,0:T(8,128)(2,1)}, bf16[64,2176]{1,0:T(8,128)(2,1)}) custom-call(bf16[128,2048]{1,0:T(8,128)(2,1)} %refs_0_.2, f32[1,2048]{1,0:T(1,128)} %bitcast.22, bf16[16,2048]{1,0:T(8,128)(2,1)} %bitcast.21, s32[8,128]{1,0:T(8,128)} %bitcast.23), custom_call_target="tpu_custom_call" | custom-call | tf_op jit(solution)/shard_map/pack_rows/pallas_call | solution.py:57
  3.2 2.6 %collective-permute-start.1 = (bf16[64,2176]{1,0:T(8,128)(2,1)}, bf16[64,2176]{1,0:T(8,128)(2,1)S(1)}, u32[]{:S(2)}, u32[]{:S(2)}) collective-permute-start(bf16[64,2176]{1,0:T(8,128)(2,1)} %get-tuple-element.47), channel_id=1, source_target_pairs={{0,4},{1,5},{4,8},{5,9},{8,12},{9,13},{12,14},{13,15},{14,10},{15,... | collective-permute-start | bytes 835592 | tf_op jit(solution)/shard_map/ppermute | solution.py:198
  5.8 1.9 %collective-permute-start.7 = (bf16[64,2176]{1,0:T(8,128)(2,1)}, bf16[64,2176]{1,0:T(8,128)(2,1)S(1)}, u32[]{:S(2)}, u32[]{:S(2)}) collective-permute-start(bf16[64,2176]{1,0:T(8,128)(2,1)} %get-tuple-element.47), channel_id=1, source_target_pairs={{0,2},{1,3},{4,0},{5,1},{8,4},{9,5},{12,8},{13,9},{14,12},{15,13},... | collective-permute-start | bytes 835592 | tf_op jit(solution)/shard_map/ppermute | solution.py:198
  7.9 1.9 %copy-done = bf16[1,2048,768]{2,1,0:T(8,128)(2,1)S(1)} copy-done((bf16[1,2048,768]{2,1,0:T(8,128)(2,1)S(1)}, bf16[1,2048,768]{2,1,0:T(8,128)(2,1)}, u32[]{:S(2)}) %copy-start) | copy-done | bytes 3145752
  9.8 1.9 %copy-done.2 = bf16[1,2048,768]{2,1,0:T(8,128)(2,1)S(1)} copy-done((bf16[1,2048,768]{2,1,0:T(8,128)(2,1)S(1)}, bf16[1,2048,768]{2,1,0:T(8,128)(2,1)}, u32[]{:S(2)}) %copy-start.2) | copy-done | bytes 3145752
  11.6 1.9 %copy-done.4 = bf16[1,768,2048]{2,1,0:T(8,128)(2,1)S(1)} copy-done((bf16[1,768,2048]{2,1,0:T(8,128)(2,1)S(1)}, bf16[1,768,2048]{2,1,0:T(8,128)(2,1)}, u32[]{:S(2)}) %copy-start.4) | copy-done | bytes 3145752
  13.6 1.9 %collective-permute-done.2.refs_3_ = bf16[64,2176]{1,0:T(8,128)(2,1)S(1)} collective-permute-done((bf16[64,2176]{1,0:T(8,128)(2,1)}, bf16[64,2176]{1,0:T(8,128)(2,1)S(1)}, u32[]{:S(2)}, u32[]{:S(2)}) %collective-permute-start.2) | collective-permute-done | bytes 278560 | tf_op jit(solution)/shard_map/ppermute | solution.py:198
  17.5 3.9 %collective-permute-done.7.refs_2_ = bf16[64,2176]{1,0:T(8,128)(2,1)S(1)} collective-permute-done((bf16[64,2176]{1,0:T(8,128)(2,1)}, bf16[64,2176]{1,0:T(8,128)(2,1)S(1)}, u32[]{:S(2)}, u32[]{:S(2)}) %collective-permute-start.7) | collective-permute-done | bytes 278560 | tf_op jit(solution)/shard_map/ppermute | solution.py:198
  21.5 2.0 %collective-permute-start.9 = (bf16[64,2176]{1,0:T(8,128)(2,1)S(1)}, bf16[64,2176]{1,0:T(8,128)(2,1)S(1)}, u32[]{:S(2)}, u32[]{:S(2)}) collective-permute-start(bf16[64,2176]{1,0:T(8,128)(2,1)S(1)} %collective-permute-done.6.refs_1_), channel_id=1, source_target_pairs={{0,4},{1,5},{4,8},{5,9},{8,12},{9,13},{12,14},{13,15},{14,10},{15,... | collective-permute-start | bytes 835592 | tf_op jit(solution)/shard_map/ppermute | solution.py:198
  23.5 3.9 %expert_ffn.5 = (bf16[128,2048]{1,0:T(8,128)(2,1)S(1)}, bf16[128,2048]{1,0:T(8,128)(2,1)S(1)}) custom-call(bf16[128,2176]{1,0:T(8,128)(2,1)S(1)} %copy-done.5, bf16[128,2176]{1,0:T(8,128)(2,1)S(1)} %collective-permute-done.refs_1_, bf16[2048,768]{1,0:T(8,128)(2,1)S(1)} %bitcast.6, bf16[2048,768]{1,0:T(8,128)(2,1)S(1)} %bitcast.11, ...), custom_call_target="tpu_custom_call" | custom-call | flops 805306368 | bytes 524288 | tf_op jit(solution)/shard_map/expert_ffn/pallas_call | solution.py:111
  27.5 1.6 %collective-permute-start.12 = (bf16[64,2176]{1,0:T(8,128)(2,1)S(1)}, bf16[64,2176]{1,0:T(8,128)(2,1)S(1)}, u32[]{:S(2)}, u32[]{:S(2)}) collective-permute-start(bf16[64,2176]{1,0:T(8,128)(2,1)S(1)} %collective-permute-done.3.refs_0_), channel_id=1, source_target_pairs={{0,4},{1,5},{4,8},{5,9},{8,12},{9,13},{12,14},{13,15},{14,10},{15,... | collective-permute-start | bytes 835592 | tf_op jit(solution)/shard_map/ppermute | solution.py:198
  29.1 3.6 %collective-permute-done.10.refs_2_ = bf16[64,2176]{1,0:T(8,128)(2,1)S(1)} collective-permute-done((bf16[64,2176]{1,0:T(8,128)(2,1)S(1)}, bf16[64,2176]{1,0:T(8,128)(2,1)S(1)}, u32[]{:S(2)}, u32[]{:S(2)}) %collective-permute-start.10) | collective-permute-done | bytes 278560 | tf_op jit(solution)/shard_map/ppermute | solution.py:198
  32.9 1.7 %collective-permute-start.16 = (bf16[64,2176]{1,0:T(8,128)(2,1)S(1)}, bf16[64,2176]{1,0:T(8,128)(2,1)S(1)}, u32[]{:S(2)}, u32[]{:S(2)}) collective-permute-start(bf16[64,2176]{1,0:T(8,128)(2,1)S(1)} %collective-permute-done.9.refs_1_), channel_id=1, source_target_pairs={{0,4},{1,5},{4,8},{5,9},{8,12},{9,13},{12,14},{13,15},{14,10},{15,... | collective-permute-start | bytes 835592 | tf_op jit(solution)/shard_map/ppermute | solution.py:198
  34.9 7.3 %collective-permute-done.17.refs_2_ = bf16[64,2176]{1,0:T(8,128)(2,1)S(1)} collective-permute-done((bf16[64,2176]{1,0:T(8,128)(2,1)S(1)}, bf16[64,2176]{1,0:T(8,128)(2,1)S(1)}, u32[]{:S(2)}, u32[]{:S(2)}) %collective-permute-start.17) | collective-permute-done | bytes 278560 | tf_op jit(solution)/shard_map/ppermute | solution.py:198
  43.1 3.4 %collective-permute-done.14.refs_3_ = bf16[64,2176]{1,0:T(8,128)(2,1)S(1)} collective-permute-done((bf16[64,2176]{1,0:T(8,128)(2,1)S(1)}, bf16[64,2176]{1,0:T(8,128)(2,1)S(1)}, u32[]{:S(2)}, u32[]{:S(2)}) %collective-permute-start.14) | collective-permute-done | bytes 278560 | tf_op jit(solution)/shard_map/ppermute | solution.py:198
  46.7 1.6 %collective-permute-start.13 = (bf16[64,2176]{1,0:T(8,128)(2,1)S(1)}, bf16[64,2176]{1,0:T(8,128)(2,1)S(1)}, u32[]{:S(2)}, u32[]{:S(2)}) collective-permute-start(bf16[64,2176]{1,0:T(8,128)(2,1)S(1)} %collective-permute-done.12.refs_0_), channel_id=1, source_target_pairs={{0,4},{1,5},{4,8},{5,9},{8,12},{9,13},{12,14},{13,15},{14,10},{15,... | collective-permute-start | bytes 835592 | tf_op jit(solution)/shard_map/ppermute | solution.py:198
  49.4 6.4 %expert_ffn.8 = (bf16[64,2048]{1,0:T(8,128)(2,1)S(1)}, bf16[64,2048]{1,0:T(8,128)(2,1)S(1)}, bf16[64,2048]{1,0:T(8,128)(2,1)S(1)}, bf16[64,2048]{1,0:T(8,128)(2,1)S(1)}, bf16[256,2048]{1,0:T(8,128)(2,1)S(1)}) custom-call(bf16[256,2176]{1,0:T(8,128)(2,1)S(1)} %join_rows.6.refs_0_, bf16[256,2176]{1,0:T(8,128)(2,1)S(1)} %collective-permute-done.18.refs_1_, ...), custom_call_target="tpu_custom_call" | custom-call | flops 1610612736 | bytes 1048576 | tf_op jit(solution)/shard_map/expert_ffn/pallas_call | solution.py:111
  59.1 3.9 %expert_ffn.9 = (bf16[64,2048]{1,0:T(8,128)(2,1)S(1)}, bf16[64,2048]{1,0:T(8,128)(2,1)S(1)}, bf16[128,2048]{1,0:T(8,128)(2,1)S(1)}) custom-call(bf16[128,2176]{1,0:T(8,128)(2,1)S(1)} %join_rows.7.refs_0_, bf16[128,2176]{1,0:T(8,128)(2,1)S(1)} %collective-permute-done.19.refs_1_, bf16[2048,768]{1,0:T(8,128)(2,1)S(1)} %bitcast.8, ...), custom_call_target="tpu_custom_call" | custom-call | flops 805306368 | bytes 524288 | tf_op jit(solution)/shard_map/expert_ffn/pallas_call | solution.py:111
  63.3 1.6 %collective-permute-start.24 = (bf16[64,2048]{1,0:T(8,128)(2,1)S(1)}, bf16[64,2048]{1,0:T(8,128)(2,1)S(1)}, u32[]{:S(2)}, u32[]{:S(2)}) collective-permute-start(bf16[64,2048]{1,0:T(8,128)(2,1)S(1)} %combine_rows.17), channel_id=1, source_target_pairs={{0,4},{1,5},{4,8},{5,9},{8,12},{9,13},{12,14},{13,15},{14,10},{15,... | collective-permute-start | bytes 786440 | tf_op jit(solution)/shard_map/ppermute | solution.py:198
  66.1 1.6 %collective-permute-start.22 = (bf16[64,2048]{1,0:T(8,128)(2,1)S(1)}, bf16[64,2048]{1,0:T(8,128)(2,1)S(1)}, u32[]{:S(2)}, u32[]{:S(2)}) collective-permute-start(bf16[64,2048]{1,0:T(8,128)(2,1)S(1)} %combine_rows.16), channel_id=1, source_target_pairs={{0,4},{1,5},{4,8},{5,9},{8,12},{9,13},{12,14},{13,15},{14,10},{15,... | collective-permute-start | bytes 786440 | tf_op jit(solution)/shard_map/ppermute | solution.py:198
  67.8 6.4 %expert_ffn.6 = (bf16[64,2048]{1,0:T(8,128)(2,1)S(1)}, bf16[64,2048]{1,0:T(8,128)(2,1)S(1)}, bf16[64,2048]{1,0:T(8,128)(2,1)S(1)}, bf16[64,2048]{1,0:T(8,128)(2,1)S(1)}, bf16[256,2048]{1,0:T(8,128)(2,1)S(1)}) custom-call(bf16[256,2176]{1,0:T(8,128)(2,1)S(1)} %join_rows.5.refs_0_, bf16[256,2176]{1,0:T(8,128)(2,1)S(1)} %collective-permute-done.11.refs_1_, ...), custom_call_target="tpu_custom_call" | custom-call | flops 1610612736 | bytes 1048576 | tf_op jit(solution)/shard_map/expert_ffn/pallas_call | solution.py:111
  74.2 6.4 %expert_ffn.7 = (bf16[64,2048]{1,0:T(8,128)(2,1)S(1)}, bf16[64,2048]{1,0:T(8,128)(2,1)S(1)}, bf16[64,2048]{1,0:T(8,128)(2,1)S(1)}, bf16[64,2048]{1,0:T(8,128)(2,1)S(1)}, bf16[256,2048]{1,0:T(8,128)(2,1)S(1)}) custom-call(bf16[256,2176]{1,0:T(8,128)(2,1)S(1)} %join_rows.4.refs_0_, bf16[256,2176]{1,0:T(8,128)(2,1)S(1)} %collective-permute-done.8.refs_1_, ...), custom_call_target="tpu_custom_call" | custom-call | flops 1610612736 | bytes 1048576 | tf_op jit(solution)/shard_map/expert_ffn/pallas_call | solution.py:111
  81.9 1.6 %collective-permute-start.33 = (bf16[64,2048]{1,0:T(8,128)(2,1)S(1)}, bf16[64,2048]{1,0:T(8,128)(2,1)S(1)}, u32[]{:S(2)}, u32[]{:S(2)}) collective-permute-start(bf16[64,2048]{1,0:T(8,128)(2,1)S(1)} %combine_rows.24), channel_id=1, source_target_pairs={{0,4},{1,5},{4,8},{5,9},{8,12},{9,13},{12,14},{13,15},{14,10},{15,... | collective-permute-start | bytes 786440 | tf_op jit(solution)/shard_map/ppermute | solution.py:198
  83.5 6.1 %collective-permute-done.28.refs_2_ = bf16[64,2048]{1,0:T(8,128)(2,1)S(1)} collective-permute-done((bf16[64,2048]{1,0:T(8,128)(2,1)S(1)}, bf16[64,2048]{1,0:T(8,128)(2,1)S(1)}, u32[]{:S(2)}, u32[]{:S(2)}) %collective-permute-start.28) | collective-permute-done | bytes 262176 | tf_op jit(solution)/shard_map/ppermute | solution.py:198
  90.3 1.6 %collective-permute-start.31 = (bf16[64,2048]{1,0:T(8,128)(2,1)S(1)}, bf16[64,2048]{1,0:T(8,128)(2,1)S(1)}, u32[]{:S(2)}, u32[]{:S(2)}) collective-permute-start(bf16[64,2048]{1,0:T(8,128)(2,1)S(1)} %combine_rows.22), channel_id=1, source_target_pairs={{0,4},{1,5},{4,8},{5,9},{8,12},{9,13},{12,14},{13,15},{14,10},{15,... | collective-permute-start | bytes 786440 | tf_op jit(solution)/shard_map/ppermute | solution.py:198
  92.1 1.6 %collective-permute-start.34 = (bf16[64,2048]{1,0:T(8,128)(2,1)S(1)}, bf16[64,2048]{1,0:T(8,128)(2,1)S(1)}, u32[]{:S(2)}, u32[]{:S(2)}) collective-permute-start(bf16[64,2048]{1,0:T(8,128)(2,1)S(1)} %combine_rows.25), channel_id=1, source_target_pairs={{0,4},{1,5},{4,8},{5,9},{8,12},{9,13},{12,14},{13,15},{14,10},{15,... | collective-permute-start | bytes 786440 | tf_op jit(solution)/shard_map/ppermute | solution.py:198
  94.3 4.7 %collective-permute-done.29.refs_2_ = bf16[64,2048]{1,0:T(8,128)(2,1)S(1)} collective-permute-done((bf16[64,2048]{1,0:T(8,128)(2,1)S(1)}, bf16[64,2048]{1,0:T(8,128)(2,1)S(1)}, u32[]{:S(2)}, u32[]{:S(2)}) %collective-permute-start.29) | collective-permute-done | bytes 262176 | tf_op jit(solution)/shard_map/ppermute | solution.py:198
  99.7 1.6 %collective-permute-start.32 = (bf16[64,2048]{1,0:T(8,128)(2,1)S(1)}, bf16[64,2048]{1,0:T(8,128)(2,1)S(1)}, u32[]{:S(2)}, u32[]{:S(2)}) collective-permute-start(bf16[64,2048]{1,0:T(8,128)(2,1)S(1)} %combine_rows.23), channel_id=1, source_target_pairs={{0,4},{1,5},{4,8},{5,9},{8,12},{9,13},{12,14},{13,15},{14,10},{15,... | collective-permute-start | bytes 786440 | tf_op jit(solution)/shard_map/ppermute | solution.py:198
  101.4 3.9 %collective-permute-done.34.refs_2_ = bf16[64,2048]{1,0:T(8,128)(2,1)S(1)} collective-permute-done((bf16[64,2048]{1,0:T(8,128)(2,1)S(1)}, bf16[64,2048]{1,0:T(8,128)(2,1)S(1)}, u32[]{:S(2)}, u32[]{:S(2)}) %collective-permute-start.34) | collective-permute-done | bytes 262176 | tf_op jit(solution)/shard_map/ppermute | solution.py:198
  105.3 1.6 %collective-permute-start.35 = (bf16[64,2048]{1,0:T(8,128)(2,1)S(1)}, bf16[64,2048]{1,0:T(8,128)(2,1)S(1)}, u32[]{:S(2)}, u32[]{:S(2)}) collective-permute-start(bf16[64,2048]{1,0:T(8,128)(2,1)S(1)} %combine_rows.26), channel_id=1, source_target_pairs={{0,4},{1,5},{4,8},{5,9},{8,12},{9,13},{12,14},{13,15},{14,10},{15,... | collective-permute-start | bytes 786440 | tf_op jit(solution)/shard_map/ppermute | solution.py:198
  107.6 2.7 %collective-permute-done.30.refs_2_ = bf16[64,2048]{1,0:T(8,128)(2,1)S(1)} collective-permute-done((bf16[64,2048]{1,0:T(8,128)(2,1)S(1)}, bf16[64,2048]{1,0:T(8,128)(2,1)S(1)}, u32[]{:S(2)}, u32[]{:S(2)}) %collective-permute-start.30) | collective-permute-done | bytes 262176 | tf_op jit(solution)/shard_map/ppermute | solution.py:198
  110.8 3.5 %collective-permute-done.35.refs_6_ = bf16[64,2048]{1,0:T(8,128)(2,1)S(1)} collective-permute-done((bf16[64,2048]{1,0:T(8,128)(2,1)S(1)}, bf16[64,2048]{1,0:T(8,128)(2,1)S(1)}, u32[]{:S(2)}, u32[]{:S(2)}) %collective-permute-start.35) | collective-permute-done | bytes 262176 | tf_op jit(solution)/shard_map/ppermute | solution.py:198
  (83 shorter events, 15.7 us)
Async XLA Ops:
  2.6 20.9 %collective-permute-start = (bf16[128,2176]{1,0:T(8,128)(2,1)}, bf16[128,2176]{1,0:T(8,128)(2,1)S(1)}, u32[]{:S(2)}, u32[]{:S(2)}) collective-permute-start(bf16[128,2176]{1,0:T(8,128)(2,1)} %get-tuple-element.46.refs_0_), channel_id=1, source_target_pairs={{0,1},{1,0},{2,3},{3,2},{4,5},{5,4},{6,7},{7,6},{8,9},{9,8},{10,11... | collective-permute-start | bytes 1671176 | tf_op jit(solution)/shard_map/ppermute | solution.py:203
  3.2 10.4 %collective-permute-start.1 = (bf16[64,2176]{1,0:T(8,128)(2,1)}, bf16[64,2176]{1,0:T(8,128)(2,1)S(1)}, u32[]{:S(2)}, u32[]{:S(2)}) collective-permute-start(bf16[64,2176]{1,0:T(8,128)(2,1)} %get-tuple-element.47), channel_id=1, source_target_pairs={{0,4},{1,5},{4,8},{5,9},{8,12},{9,13},{12,14},{13,15},{14,10},{15,... | collective-permute-start | bytes 835592 | tf_op jit(solution)/shard_map/ppermute | solution.py:198
  5.8 9.7 %collective-permute-start.2 = (bf16[64,2176]{1,0:T(8,128)(2,1)}, bf16[64,2176]{1,0:T(8,128)(2,1)S(1)}, u32[]{:S(2)}, u32[]{:S(2)}) collective-permute-start(bf16[64,2176]{1,0:T(8,128)(2,1)} %get-tuple-element.48), channel_id=1, source_target_pairs={{0,2},{1,3},{4,0},{5,1},{8,4},{9,5},{12,8},{13,9},{14,12},{15,13},... | collective-permute-start | bytes 835592 | tf_op jit(solution)/shard_map/ppermute | solution.py:198
  5.8 15.7 %collective-permute-start.7 = (bf16[64,2176]{1,0:T(8,128)(2,1)}, bf16[64,2176]{1,0:T(8,128)(2,1)S(1)}, u32[]{:S(2)}, u32[]{:S(2)}) collective-permute-start(bf16[64,2176]{1,0:T(8,128)(2,1)} %get-tuple-element.47), channel_id=1, source_target_pairs={{0,2},{1,3},{4,0},{5,1},{8,4},{9,5},{12,8},{13,9},{14,12},{15,13},... | collective-permute-start | bytes 835592 | tf_op jit(solution)/shard_map/ppermute | solution.py:198
  7.8 13.7 %collective-permute-start.6 = (bf16[64,2176]{1,0:T(8,128)(2,1)}, bf16[64,2176]{1,0:T(8,128)(2,1)S(1)}, u32[]{:S(2)}, u32[]{:S(2)}) collective-permute-start(bf16[64,2176]{1,0:T(8,128)(2,1)} %get-tuple-element.48), channel_id=1, source_target_pairs={{0,4},{1,5},{4,8},{5,9},{8,12},{9,13},{12,14},{13,15},{14,10},{15,... | collective-permute-start | bytes 835592 | tf_op jit(solution)/shard_map/ppermute | solution.py:198
  15.5 11.9 %collective-permute-start.3 = (bf16[64,2176]{1,0:T(8,128)(2,1)S(1)}, bf16[64,2176]{1,0:T(8,128)(2,1)S(1)}, u32[]{:S(2)}, u32[]{:S(2)}) collective-permute-start(bf16[64,2176]{1,0:T(8,128)(2,1)S(1)} %collective-permute-done.1.refs_0_), channel_id=1, source_target_pairs={{0,4},{1,5},{4,8},{5,9},{8,12},{9,13},{12,14},{13,15},{14,10},{15,... | collective-permute-start | bytes 835592 | tf_op jit(solution)/shard_map/ppermute | solution.py:198
  17.1 10.4 %collective-permute-start.4 = (bf16[64,2176]{1,0:T(8,128)(2,1)S(1)}, bf16[64,2176]{1,0:T(8,128)(2,1)S(1)}, u32[]{:S(2)}, u32[]{:S(2)}) collective-permute-start(bf16[64,2176]{1,0:T(8,128)(2,1)S(1)} %collective-permute-done.2.refs_3_), channel_id=1, source_target_pairs={{0,2},{1,3},{4,0},{5,1},{8,4},{9,5},{12,8},{13,9},{14,12},{15,13},... | collective-permute-start | bytes 835592 | tf_op jit(solution)/shard_map/ppermute | solution.py:198
  21.5 11.2 %collective-permute-start.10 = (bf16[64,2176]{1,0:T(8,128)(2,1)S(1)}, bf16[64,2176]{1,0:T(8,128)(2,1)S(1)}, u32[]{:S(2)}, u32[]{:S(2)}) collective-permute-start(bf16[64,2176]{1,0:T(8,128)(2,1)S(1)} %collective-permute-done.7.refs_2_), channel_id=1, source_target_pairs={{0,2},{1,3},{4,0},{5,1},{8,4},{9,5},{12,8},{13,9},{14,12},{15,13},... | collective-permute-start | bytes 835592 | tf_op jit(solution)/shard_map/ppermute | solution.py:198
  21.5 11.4 %collective-permute-start.9 = (bf16[64,2176]{1,0:T(8,128)(2,1)S(1)}, bf16[64,2176]{1,0:T(8,128)(2,1)S(1)}, u32[]{:S(2)}, u32[]{:S(2)}) collective-permute-start(bf16[64,2176]{1,0:T(8,128)(2,1)S(1)} %collective-permute-done.6.refs_1_), channel_id=1, source_target_pairs={{0,4},{1,5},{4,8},{5,9},{8,12},{9,13},{12,14},{13,15},{14,10},{15,... | collective-permute-start | bytes 835592 | tf_op jit(solution)/shard_map/ppermute | solution.py:198
  27.5 15.6 %collective-permute-start.12 = (bf16[64,2176]{1,0:T(8,128)(2,1)S(1)}, bf16[64,2176]{1,0:T(8,128)(2,1)S(1)}, u32[]{:S(2)}, u32[]{:S(2)}) collective-permute-start(bf16[64,2176]{1,0:T(8,128)(2,1)S(1)} %collective-permute-done.3.refs_0_), channel_id=1, source_target_pairs={{0,4},{1,5},{4,8},{5,9},{8,12},{9,13},{12,14},{13,15},{14,10},{15,... | collective-permute-start | bytes 835592 | tf_op jit(solution)/shard_map/ppermute | solution.py:198
  32.6 9.6 %collective-permute-start.17 = (bf16[64,2176]{1,0:T(8,128)(2,1)S(1)}, bf16[64,2176]{1,0:T(8,128)(2,1)S(1)}, u32[]{:S(2)}, u32[]{:S(2)}) collective-permute-start(bf16[64,2176]{1,0:T(8,128)(2,1)S(1)} %collective-permute-done.10.refs_2_), channel_id=1, source_target_pairs={{0,2},{1,3},{4,0},{5,1},{8,4},{9,5},{12,8},{13,9},{14,12},{15,13},... | collective-permute-start | bytes 835592 | tf_op jit(solution)/shard_map/ppermute | solution.py:198
  32.9 10.1 %collective-permute-start.16 = (bf16[64,2176]{1,0:T(8,128)(2,1)S(1)}, bf16[64,2176]{1,0:T(8,128)(2,1)S(1)}, u32[]{:S(2)}, u32[]{:S(2)}) collective-permute-start(bf16[64,2176]{1,0:T(8,128)(2,1)S(1)} %collective-permute-done.9.refs_1_), channel_id=1, source_target_pairs={{0,4},{1,5},{4,8},{5,9},{8,12},{9,13},{12,14},{13,15},{14,10},{15,... | collective-permute-start | bytes 835592 | tf_op jit(solution)/shard_map/ppermute | solution.py:198
  34.7 11.8 %collective-permute-start.14 = (bf16[64,2176]{1,0:T(8,128)(2,1)S(1)}, bf16[64,2176]{1,0:T(8,128)(2,1)S(1)}, u32[]{:S(2)}, u32[]{:S(2)}) collective-permute-start(bf16[64,2176]{1,0:T(8,128)(2,1)S(1)} %collective-permute-done.4.refs_3_), channel_id=1, source_target_pairs={{0,2},{1,3},{4,0},{5,1},{8,4},{9,5},{12,8},{13,9},{14,12},{15,13},... | collective-permute-start | bytes 835592 | tf_op jit(solution)/shard_map/ppermute | solution.py:198
  46.7 9.1 %collective-permute-start.13 = (bf16[64,2176]{1,0:T(8,128)(2,1)S(1)}, bf16[64,2176]{1,0:T(8,128)(2,1)S(1)}, u32[]{:S(2)}, u32[]{:S(2)}) collective-permute-start(bf16[64,2176]{1,0:T(8,128)(2,1)S(1)} %collective-permute-done.12.refs_0_), channel_id=1, source_target_pairs={{0,4},{1,5},{4,8},{5,9},{8,12},{9,13},{12,14},{13,15},{14,10},{15,... | collective-permute-start | bytes 835592 | tf_op jit(solution)/shard_map/ppermute | solution.py:198
  48.3 8.7 %collective-permute-start.15 = (bf16[64,2176]{1,0:T(8,128)(2,1)S(1)}, bf16[64,2176]{1,0:T(8,128)(2,1)S(1)}, u32[]{:S(2)}, u32[]{:S(2)}) collective-permute-start(bf16[64,2176]{1,0:T(8,128)(2,1)S(1)} %collective-permute-done.14.refs_3_), channel_id=1, source_target_pairs={{0,2},{1,3},{4,0},{5,1},{8,4},{9,5},{12,8},{13,9},{14,12},{15,13},... | collective-permute-start | bytes 835592 | tf_op jit(solution)/shard_map/ppermute | solution.py:198
  57.2 8.9 %collective-permute-start.11 = (bf16[256,2176]{1,0:T(8,128)(2,1)S(1)}, bf16[256,2176]{1,0:T(8,128)(2,1)S(1)}, u32[]{:S(2)}, u32[]{:S(2)}) collective-permute-start(bf16[256,2176]{1,0:T(8,128)(2,1)S(1)} %join_rows.5.refs_0_), channel_id=1, source_target_pairs={{0,1},{1,0},{2,3},{3,2},{4,5},{5,4},{6,7},{7,6},{8,9},{9,8},{10,11... | collective-permute-start | bytes 3342344 | tf_op jit(solution)/shard_map/ppermute | solution.py:203
  57.9 16.2 %collective-permute-start.8 = (bf16[256,2176]{1,0:T(8,128)(2,1)S(1)}, bf16[256,2176]{1,0:T(8,128)(2,1)S(1)}, u32[]{:S(2)}, u32[]{:S(2)}) collective-permute-start(bf16[256,2176]{1,0:T(8,128)(2,1)S(1)} %join_rows.4.refs_0_), channel_id=1, source_target_pairs={{0,1},{1,0},{2,3},{3,2},{4,5},{5,4},{6,7},{7,6},{8,9},{9,8},{10,11... | collective-permute-start | bytes 3342344 | tf_op jit(solution)/shard_map/ppermute | solution.py:203
  63.3 17.3 %collective-permute-start.24 = (bf16[64,2048]{1,0:T(8,128)(2,1)S(1)}, bf16[64,2048]{1,0:T(8,128)(2,1)S(1)}, u32[]{:S(2)}, u32[]{:S(2)}) collective-permute-start(bf16[64,2048]{1,0:T(8,128)(2,1)S(1)} %combine_rows.17), channel_id=1, source_target_pairs={{0,4},{1,5},{4,8},{5,9},{8,12},{9,13},{12,14},{13,15},{14,10},{15,... | collective-permute-start | bytes 786440 | tf_op jit(solution)/shard_map/ppermute | solution.py:198
  65.0 15.6 %collective-permute-start.25 = (bf16[64,2048]{1,0:T(8,128)(2,1)S(1)}, bf16[64,2048]{1,0:T(8,128)(2,1)S(1)}, u32[]{:S(2)}, u32[]{:S(2)}) collective-permute-start(bf16[64,2048]{1,0:T(8,128)(2,1)S(1)} %combine_rows.18), channel_id=1, source_target_pairs={{0,2},{1,3},{4,0},{5,1},{8,4},{9,5},{12,8},{13,9},{14,12},{15,13},... | collective-permute-start | bytes 786440 | tf_op jit(solution)/shard_map/ppermute | solution.py:198
  65.6 15.0 %collective-permute-start.21 = (bf16[64,2048]{1,0:T(8,128)(2,1)S(1)}, bf16[64,2048]{1,0:T(8,128)(2,1)S(1)}, u32[]{:S(2)}, u32[]{:S(2)}) collective-permute-start(bf16[64,2048]{1,0:T(8,128)(2,1)S(1)} %combine_rows.15), channel_id=1, source_target_pairs={{0,2},{1,3},{4,0},{5,1},{8,4},{9,5},{12,8},{13,9},{14,12},{15,13},... | collective-permute-start | bytes 786440 | tf_op jit(solution)/shard_map/ppermute | solution.py:198
  66.1 14.5 %collective-permute-start.22 = (bf16[64,2048]{1,0:T(8,128)(2,1)S(1)}, bf16[64,2048]{1,0:T(8,128)(2,1)S(1)}, u32[]{:S(2)}, u32[]{:S(2)}) collective-permute-start(bf16[64,2048]{1,0:T(8,128)(2,1)S(1)} %combine_rows.16), channel_id=1, source_target_pairs={{0,4},{1,5},{4,8},{5,9},{8,12},{9,13},{12,14},{13,15},{14,10},{15,... | collective-permute-start | bytes 786440 | tf_op jit(solution)/shard_map/ppermute | solution.py:198
  80.6 9.0 %collective-permute-start.27 = (bf16[256,2048]{1,0:T(8,128)(2,1)S(1)}, bf16[256,2048]{1,0:T(8,128)(2,1)S(1)}, u32[]{:S(2)}, u32[]{:S(2)}) collective-permute-start(bf16[256,2048]{1,0:T(8,128)(2,1)S(1)} %get-tuple-element.74), channel_id=1, source_target_pairs={{0,1},{1,0},{2,3},{3,2},{4,5},{5,4},{6,7},{7,6},{8,9},{9,8},{10,11... | collective-permute-start | bytes 3145736 | tf_op jit(solution)/shard_map/ppermute | solution.py:203
  80.7 13.1 %collective-permute-start.26 = (bf16[256,2048]{1,0:T(8,128)(2,1)S(1)}, bf16[256,2048]{1,0:T(8,128)(2,1)S(1)}, u32[]{:S(2)}, u32[]{:S(2)}) collective-permute-start(bf16[256,2048]{1,0:T(8,128)(2,1)S(1)} %get-tuple-element.72), channel_id=1, source_target_pairs={{0,1},{1,0},{2,3},{3,2},{4,5},{5,4},{6,7},{7,6},{8,9},{9,8},{10,11... | collective-permute-start | bytes 3145736 | tf_op jit(solution)/shard_map/ppermute | solution.py:203
  81.9 10.1 %collective-permute-start.33 = (bf16[64,2048]{1,0:T(8,128)(2,1)S(1)}, bf16[64,2048]{1,0:T(8,128)(2,1)S(1)}, u32[]{:S(2)}, u32[]{:S(2)}) collective-permute-start(bf16[64,2048]{1,0:T(8,128)(2,1)S(1)} %combine_rows.24), channel_id=1, source_target_pairs={{0,4},{1,5},{4,8},{5,9},{8,12},{9,13},{12,14},{13,15},{14,10},{15,... | collective-permute-start | bytes 786440 | tf_op jit(solution)/shard_map/ppermute | solution.py:198
  83.5 24.1 %collective-permute-start.5 = (bf16[128,2048]{1,0:T(8,128)(2,1)S(1)}, bf16[128,2048]{1,0:T(8,128)(2,1)S(1)}, u32[]{:S(2)}, u32[]{:S(2)}) collective-permute-start(bf16[128,2048]{1,0:T(8,128)(2,1)S(1)} %get-tuple-element.54), channel_id=1, source_target_pairs={{0,1},{1,0},{2,3},{3,2},{4,5},{5,4},{6,7},{7,6},{8,9},{9,8},{10,11... | collective-permute-start | bytes 1572872 | tf_op jit(solution)/shard_map/ppermute | solution.py:203
  89.7 9.3 %collective-permute-start.29 = (bf16[64,2048]{1,0:T(8,128)(2,1)S(1)}, bf16[64,2048]{1,0:T(8,128)(2,1)S(1)}, u32[]{:S(2)}, u32[]{:S(2)}) collective-permute-start(bf16[64,2048]{1,0:T(8,128)(2,1)S(1)} %combine_rows.20), channel_id=1, source_target_pairs={{0,2},{1,3},{4,0},{5,1},{8,4},{9,5},{12,8},{13,9},{14,12},{15,13},... | collective-permute-start | bytes 786440 | tf_op jit(solution)/shard_map/ppermute | solution.py:198
  90.3 9.3 %collective-permute-start.31 = (bf16[64,2048]{1,0:T(8,128)(2,1)S(1)}, bf16[64,2048]{1,0:T(8,128)(2,1)S(1)}, u32[]{:S(2)}, u32[]{:S(2)}) collective-permute-start(bf16[64,2048]{1,0:T(8,128)(2,1)S(1)} %combine_rows.22), channel_id=1, source_target_pairs={{0,4},{1,5},{4,8},{5,9},{8,12},{9,13},{12,14},{13,15},{14,10},{15,... | collective-permute-start | bytes 786440 | tf_op jit(solution)/shard_map/ppermute | solution.py:198
  92.1 13.2 %collective-permute-start.34 = (bf16[64,2048]{1,0:T(8,128)(2,1)S(1)}, bf16[64,2048]{1,0:T(8,128)(2,1)S(1)}, u32[]{:S(2)}, u32[]{:S(2)}) collective-permute-start(bf16[64,2048]{1,0:T(8,128)(2,1)S(1)} %combine_rows.25), channel_id=1, source_target_pairs={{0,4},{1,5},{4,8},{5,9},{8,12},{9,13},{12,14},{13,15},{14,10},{15,... | collective-permute-start | bytes 786440 | tf_op jit(solution)/shard_map/ppermute | solution.py:198
  93.8 13.2 %collective-permute-start.36 = (bf16[64,2048]{1,0:T(8,128)(2,1)S(1)}, bf16[64,2048]{1,0:T(8,128)(2,1)S(1)}, u32[]{:S(2)}, u32[]{:S(2)}) collective-permute-start(bf16[64,2048]{1,0:T(8,128)(2,1)S(1)} %combine_rows.27), channel_id=1, source_target_pairs={{0,2},{1,3},{4,0},{5,1},{8,4},{9,5},{12,8},{13,9},{14,12},{15,13},... | collective-permute-start | bytes 786440 | tf_op jit(solution)/shard_map/ppermute | solution.py:198
  99.1 11.1 %collective-permute-start.30 = (bf16[64,2048]{1,0:T(8,128)(2,1)S(1)}, bf16[64,2048]{1,0:T(8,128)(2,1)S(1)}, u32[]{:S(2)}, u32[]{:S(2)}) collective-permute-start(bf16[64,2048]{1,0:T(8,128)(2,1)S(1)} %combine_rows.21), channel_id=1, source_target_pairs={{0,2},{1,3},{4,0},{5,1},{8,4},{9,5},{12,8},{13,9},{14,12},{15,13},... | collective-permute-start | bytes 786440 | tf_op jit(solution)/shard_map/ppermute | solution.py:198
  99.7 11.1 %collective-permute-start.32 = (bf16[64,2048]{1,0:T(8,128)(2,1)S(1)}, bf16[64,2048]{1,0:T(8,128)(2,1)S(1)}, u32[]{:S(2)}, u32[]{:S(2)}) collective-permute-start(bf16[64,2048]{1,0:T(8,128)(2,1)S(1)} %combine_rows.23), channel_id=1, source_target_pairs={{0,4},{1,5},{4,8},{5,9},{8,12},{9,13},{12,14},{13,15},{14,10},{15,... | collective-permute-start | bytes 786440 | tf_op jit(solution)/shard_map/ppermute | solution.py:198
  105.3 9.1 %collective-permute-start.35 = (bf16[64,2048]{1,0:T(8,128)(2,1)S(1)}, bf16[64,2048]{1,0:T(8,128)(2,1)S(1)}, u32[]{:S(2)}, u32[]{:S(2)}) collective-permute-start(bf16[64,2048]{1,0:T(8,128)(2,1)S(1)} %combine_rows.26), channel_id=1, source_target_pairs={{0,4},{1,5},{4,8},{5,9},{8,12},{9,13},{12,14},{13,15},{14,10},{15,... | collective-permute-start | bytes 786440 | tf_op jit(solution)/shard_map/ppermute | solution.py:198
  (12 other events, 64.0 us)

commit v3 on v0

--- a/solution.py
+++ b/solution.py
@@ -249,6 +249,8 @@
             own_came = sibling(sent)
         else:
             long_a[k], long_b[k] = beside((long_a[k], long_b[k]), k - 2 if k <= full else full)
+            if k == full:
+                long_a[k], own_came = tie((long_a[k], own_came))
     far = join([long_a[-1], long_b[-1]])
     far_a, far_b, sent = near(far, sibling(far), 2)
 

time: 114 us -> 115 us (level)
  transfers between devices with their start and end apart: 38 -> 38, of which waited for: 20 -> 21; matrix products, arithmetic and copies ran while one was open for 0% -> 0% of each run, Pallas kernels for 25% -> 25%
where the time goes in v3:
time: 115 us
  waiting for transfers between devices  44.8 us (39%)
  Pallas kernels  32.2 us (28%)
  starting transfers between devices  31.8 us (28%)
  local copies, waits for them, and re-layouts  5.68 us (5%)
    ppermute x28, waiting for transfers between devices, shift(): return lambda x: lax.ppermute(x, 'expert', pairs)  42.9 us
    ppermute x28, starting transfers between devices, shift(): return lambda x: lax.ppermute(x, 'expert', pairs)  29.8 us
    pallas_call x5, Pallas kernels, ffn(): pl.pallas_call(functools.partial(ffn_kernel, heights, splits), out_shape=...  27 us
    unnamed x12, local copies, waits for them, and re-layouts  5.68 us
    pallas_call x1, Pallas kernels, pack(): pl.pallas_call(pack_kernel, out_shape=[jax.ShapeDtypeStruct((r, width + l...  2.62 us
  transfers between devices with their start and end apart: 38, of which 21 were waited for; matrix products, arithmetic and copies ran while one was open for 0% of the time, Pallas kernels for 25%

profile of v3, /device:TPU:0, one launch (start us, length us, event | category | flops | bytes accessed | tf_op | source)
XLA Modules:
  0.0 114.7 jit_solution(13122769093961305027)
XLA Ops:
  0.0 2.6 %pack_rows.1 = (bf16[128,2176]{1,0:T(8,128)(2,1)}, bf16[64,2176]{1,0:T(8,128)(2,1)}, bf16[64,2176]{1,0:T(8,128)(2,1)}) custom-call(bf16[128,2048]{1,0:T(8,128)(2,1)} %refs_0_.2, f32[1,2048]{1,0:T(1,128)} %bitcast.22, bf16[16,2048]{1,0:T(8,128)(2,1)} %bitcast.21, s32[8,128]{1,0:T(8,128)} %bitcast.23), custom_call_target="tpu_custom_call" | custom-call | tf_op jit(solution)/shard_map/pack_rows/pallas_call | solution.py:57
  2.6 3.1 %collective-permute-start.1 = (bf16[64,2176]{1,0:T(8,128)(2,1)}, bf16[64,2176]{1,0:T(8,128)(2,1)S(1)}, u32[]{:S(2)}, u32[]{:S(2)}) collective-permute-start(bf16[64,2176]{1,0:T(8,128)(2,1)} %get-tuple-element.48), channel_id=1, source_target_pairs={{0,4},{1,5},{4,8},{5,9},{8,12},{9,13},{12,14},{13,15},{14,10},{15,... | collective-permute-start | bytes 835592 | tf_op jit(solution)/shard_map/ppermute | solution.py:198
  5.7 2.0 %collective-permute-start.7 = (bf16[64,2176]{1,0:T(8,128)(2,1)}, bf16[64,2176]{1,0:T(8,128)(2,1)S(1)}, u32[]{:S(2)}, u32[]{:S(2)}) collective-permute-start(bf16[64,2176]{1,0:T(8,128)(2,1)} %get-tuple-element.49), channel_id=1, source_target_pairs={{0,4},{1,5},{4,8},{5,9},{8,12},{9,13},{12,14},{13,15},{14,10},{15,... | collective-permute-start | bytes 835592 | tf_op jit(solution)/shard_map/ppermute | solution.py:198
  7.8 1.9 %copy-done = bf16[1,2048,768]{2,1,0:T(8,128)(2,1)S(1)} copy-done((bf16[1,2048,768]{2,1,0:T(8,128)(2,1)S(1)}, bf16[1,2048,768]{2,1,0:T(8,128)(2,1)}, u32[]{:S(2)}) %copy-start) | copy-done | bytes 3145752
  9.6 1.9 %copy-done.2 = bf16[1,2048,768]{2,1,0:T(8,128)(2,1)S(1)} copy-done((bf16[1,2048,768]{2,1,0:T(8,128)(2,1)S(1)}, bf16[1,2048,768]{2,1,0:T(8,128)(2,1)}, u32[]{:S(2)}) %copy-start.2) | copy-done | bytes 3145752
  11.5 1.9 %copy-done.4 = bf16[1,768,2048]{2,1,0:T(8,128)(2,1)S(1)} copy-done((bf16[1,768,2048]{2,1,0:T(8,128)(2,1)S(1)}, bf16[1,768,2048]{2,1,0:T(8,128)(2,1)}, u32[]{:S(2)}) %copy-start.4) | copy-done | bytes 3145752
  13.4 2.1 %collective-permute-done.2.refs_3_ = bf16[64,2176]{1,0:T(8,128)(2,1)S(1)} collective-permute-done((bf16[64,2176]{1,0:T(8,128)(2,1)}, bf16[64,2176]{1,0:T(8,128)(2,1)S(1)}, u32[]{:S(2)}, u32[]{:S(2)}) %collective-permute-start.2) | collective-permute-done | bytes 278560 | tf_op jit(solution)/shard_map/ppermute | solution.py:198
  15.5 3.0 %collective-permute-done.7.refs_1_ = bf16[64,2176]{1,0:T(8,128)(2,1)S(1)} collective-permute-done((bf16[64,2176]{1,0:T(8,128)(2,1)}, bf16[64,2176]{1,0:T(8,128)(2,1)S(1)}, u32[]{:S(2)}, u32[]{:S(2)}) %collective-permute-start.7) | collective-permute-done | bytes 278560 | tf_op jit(solution)/shard_map/ppermute | solution.py:198
  20.7 1.6 %collective-permute-start.3 = (bf16[64,2176]{1,0:T(8,128)(2,1)S(1)}, bf16[64,2176]{1,0:T(8,128)(2,1)S(1)}, u32[]{:S(2)}, u32[]{:S(2)}) collective-permute-start(bf16[64,2176]{1,0:T(8,128)(2,1)S(1)} %collective-permute-done.1.refs_0_), channel_id=1, source_target_pairs={{0,4},{1,5},{4,8},{5,9},{8,12},{9,13},{12,14},{13,15},{14,10},{15,... | collective-permute-start | bytes 835592 | tf_op jit(solution)/shard_map/ppermute | solution.py:198
  24.7 3.9 %expert_ffn.5 = (bf16[128,2048]{1,0:T(8,128)(2,1)S(1)}, bf16[128,2048]{1,0:T(8,128)(2,1)S(1)}) custom-call(bf16[128,2176]{1,0:T(8,128)(2,1)S(1)} %copy-done.5, bf16[128,2176]{1,0:T(8,128)(2,1)S(1)} %collective-permute-done.refs_1_, bf16[2048,768]{1,0:T(8,128)(2,1)S(1)} %bitcast.6, bf16[2048,768]{1,0:T(8,128)(2,1)S(1)} %bitcast.11, ...), custom_call_target="tpu_custom_call" | custom-call | flops 2415919104 | bytes 524288 | tf_op jit(solution)/shard_map/expert_ffn/pallas_call | solution.py:111
  30.2 1.6 %collective-permute-done.4.refs_3_ = bf16[64,2176]{1,0:T(8,128)(2,1)S(1)} collective-permute-done((bf16[64,2176]{1,0:T(8,128)(2,1)S(1)}, bf16[64,2176]{1,0:T(8,128)(2,1)S(1)}, u32[]{:S(2)}, u32[]{:S(2)}) %collective-permute-start.4) | collective-permute-done | bytes 278560 | tf_op jit(solution)/shard_map/ppermute | solution.py:198
  33.4 2.2 %collective-permute-done.12.refs_1_ = bf16[64,2176]{1,0:T(8,128)(2,1)S(1)} collective-permute-done((bf16[64,2176]{1,0:T(8,128)(2,1)S(1)}, bf16[64,2176]{1,0:T(8,128)(2,1)S(1)}, u32[]{:S(2)}, u32[]{:S(2)}) %collective-permute-start.12) | collective-permute-done | bytes 278560 | tf_op jit(solution)/shard_map/ppermute | solution.py:198
  38.6 6.4 %expert_ffn.6 = (bf16[64,2048]{1,0:T(8,128)(2,1)S(1)}, bf16[64,2048]{1,0:T(8,128)(2,1)S(1)}, bf16[64,2048]{1,0:T(8,128)(2,1)S(1)}, bf16[64,2048]{1,0:T(8,128)(2,1)S(1)}, bf16[256,2048]{1,0:T(8,128)(2,1)S(1)}) custom-call(bf16[256,2176]{1,0:T(8,128)(2,1)S(1)} %join_rows.4.refs_0_, bf16[256,2176]{1,0:T(8,128)(2,1)S(1)} %collective-permute-done.9.refs_1_, ...), custom_call_target="tpu_custom_call" | custom-call | flops 4831838208 | bytes 1048576 | tf_op jit(solution)/shard_map/expert_ffn/pallas_call | solution.py:111
  45.2 2.0 %collective-permute-done.17.refs_1_ = bf16[64,2176]{1,0:T(8,128)(2,1)S(1)} collective-permute-done((bf16[64,2176]{1,0:T(8,128)(2,1)S(1)}, bf16[64,2176]{1,0:T(8,128)(2,1)S(1)}, u32[]{:S(2)}, u32[]{:S(2)}) %collective-permute-start.17) | collective-permute-done | bytes 278560 | tf_op jit(solution)/shard_map/ppermute | solution.py:198
  47.2 1.8 %collective-permute-done.18.refs_2_ = bf16[64,2176]{1,0:T(8,128)(2,1)S(1)} collective-permute-done((bf16[64,2176]{1,0:T(8,128)(2,1)S(1)}, bf16[64,2176]{1,0:T(8,128)(2,1)S(1)}, u32[]{:S(2)}, u32[]{:S(2)}) %collective-permute-start.18) | collective-permute-done | bytes 278560 | tf_op jit(solution)/shard_map/ppermute | solution.py:198
  49.2 1.6 %collective-permute-start.15 = (bf16[64,2176]{1,0:T(8,128)(2,1)S(1)}, bf16[64,2176]{1,0:T(8,128)(2,1)S(1)}, u32[]{:S(2)}, u32[]{:S(2)}) collective-permute-start(bf16[64,2176]{1,0:T(8,128)(2,1)S(1)} %collective-permute-done.5.refs_0_), channel_id=1, source_target_pairs={{0,4},{1,5},{4,8},{5,9},{8,12},{9,13},{12,14},{13,15},{14,10},{15,... | collective-permute-start | bytes 835592 | tf_op jit(solution)/shard_map/ppermute | solution.py:198
  52.0 6.4 %expert_ffn.8 = (bf16[64,2048]{1,0:T(8,128)(2,1)S(1)}, bf16[64,2048]{1,0:T(8,128)(2,1)S(1)}, bf16[64,2048]{1,0:T(8,128)(2,1)S(1)}, bf16[64,2048]{1,0:T(8,128)(2,1)S(1)}, bf16[256,2048]{1,0:T(8,128)(2,1)S(1)}) custom-call(bf16[256,2176]{1,0:T(8,128)(2,1)S(1)} %join_rows.6.refs_0_, bf16[256,2176]{1,0:T(8,128)(2,1)S(1)} %collective-permute-done.19.refs_1_, ...), custom_call_target="tpu_custom_call" | custom-call | flops 4831838208 | bytes 1048576 | tf_op jit(solution)/shard_map/expert_ffn/pallas_call | solution.py:111
  61.6 3.9 %expert_ffn.9 = (bf16[64,2048]{1,0:T(8,128)(2,1)S(1)}, bf16[64,2048]{1,0:T(8,128)(2,1)S(1)}, bf16[128,2048]{1,0:T(8,128)(2,1)S(1)}) custom-call(bf16[128,2176]{1,0:T(8,128)(2,1)S(1)} %join_rows.7.refs_0_, bf16[128,2176]{1,0:T(8,128)(2,1)S(1)} %collective-permute-done.20.refs_1_, bf16[2048,768]{1,0:T(8,128)(2,1)S(1)} %bitcast.9, ...), custom_call_target="tpu_custom_call" | custom-call | flops 2415919104 | bytes 524288 | tf_op jit(solution)/shard_map/expert_ffn/pallas_call | solution.py:111
  66.4 1.6 %collective-permute-start.25 = (bf16[64,2048]{1,0:T(8,128)(2,1)S(1)}, bf16[64,2048]{1,0:T(8,128)(2,1)S(1)}, u32[]{:S(2)}, u32[]{:S(2)}) collective-permute-start(bf16[64,2048]{1,0:T(8,128)(2,1)S(1)} %combine_rows.17), channel_id=1, source_target_pairs={{0,4},{1,5},{4,8},{5,9},{8,12},{9,13},{12,14},{13,15},{14,10},{15,... | collective-permute-start | bytes 786440 | tf_op jit(solution)/shard_map/ppermute | solution.py:198
  68.1 1.6 %collective-permute-start.23 = (bf16[64,2048]{1,0:T(8,128)(2,1)S(1)}, bf16[64,2048]{1,0:T(8,128)(2,1)S(1)}, u32[]{:S(2)}, u32[]{:S(2)}) collective-permute-start(bf16[64,2048]{1,0:T(8,128)(2,1)S(1)} %combine_rows.16), channel_id=1, source_target_pairs={{0,4},{1,5},{4,8},{5,9},{8,12},{9,13},{12,14},{13,15},{14,10},{15,... | collective-permute-start | bytes 786440 | tf_op jit(solution)/shard_map/ppermute | solution.py:198
  70.3 6.4 %expert_ffn.7 = (bf16[64,2048]{1,0:T(8,128)(2,1)S(1)}, bf16[64,2048]{1,0:T(8,128)(2,1)S(1)}, bf16[64,2048]{1,0:T(8,128)(2,1)S(1)}, bf16[64,2048]{1,0:T(8,128)(2,1)S(1)}, bf16[256,2048]{1,0:T(8,128)(2,1)S(1)}) custom-call(bf16[256,2176]{1,0:T(8,128)(2,1)S(1)} %join_rows.5.refs_0_, bf16[256,2176]{1,0:T(8,128)(2,1)S(1)} %collective-permute-done.14.refs_1_, ...), custom_call_target="tpu_custom_call" | custom-call | flops 4831838208 | bytes 1048576 | tf_op jit(solution)/shard_map/expert_ffn/pallas_call | solution.py:111
  76.7 3.6 %collective-permute-done.23.refs_2_ = bf16[64,2048]{1,0:T(8,128)(2,1)S(1)} collective-permute-done((bf16[64,2048]{1,0:T(8,128)(2,1)S(1)}, bf16[64,2048]{1,0:T(8,128)(2,1)S(1)}, u32[]{:S(2)}, u32[]{:S(2)}) %collective-permute-start.23) | collective-permute-done | bytes 262176 | tf_op jit(solution)/shard_map/ppermute | solution.py:198
  81.0 1.6 %collective-permute-start.33 = (bf16[64,2048]{1,0:T(8,128)(2,1)S(1)}, bf16[64,2048]{1,0:T(8,128)(2,1)S(1)}, u32[]{:S(2)}, u32[]{:S(2)}) collective-permute-start(bf16[64,2048]{1,0:T(8,128)(2,1)S(1)} %combine_rows.24), channel_id=1, source_target_pairs={{0,4},{1,5},{4,8},{5,9},{8,12},{9,13},{12,14},{13,15},{14,10},{15,... | collective-permute-start | bytes 786440 | tf_op jit(solution)/shard_map/ppermute | solution.py:198
  83.7 5.5 %collective-permute-done.33.refs_2_ = bf16[64,2048]{1,0:T(8,128)(2,1)S(1)} collective-permute-done((bf16[64,2048]{1,0:T(8,128)(2,1)S(1)}, bf16[64,2048]{1,0:T(8,128)(2,1)S(1)}, u32[]{:S(2)}, u32[]{:S(2)}) %collective-permute-start.33) | collective-permute-done | bytes 262176 | tf_op jit(solution)/shard_map/ppermute | solution.py:198
  89.3 1.6 %collective-permute-start.34 = (bf16[64,2048]{1,0:T(8,128)(2,1)S(1)}, bf16[64,2048]{1,0:T(8,128)(2,1)S(1)}, u32[]{:S(2)}, u32[]{:S(2)}) collective-permute-start(bf16[64,2048]{1,0:T(8,128)(2,1)S(1)} %combine_rows.25), channel_id=1, source_target_pairs={{0,4},{1,5},{4,8},{5,9},{8,12},{9,13},{12,14},{13,15},{14,10},{15,... | collective-permute-start | bytes 786440 | tf_op jit(solution)/shard_map/ppermute | solution.py:198
  91.1 1.6 %collective-permute-start.31 = (bf16[64,2048]{1,0:T(8,128)(2,1)S(1)}, bf16[64,2048]{1,0:T(8,128)(2,1)S(1)}, u32[]{:S(2)}, u32[]{:S(2)}) collective-permute-start(bf16[64,2048]{1,0:T(8,128)(2,1)S(1)} %combine_rows.22), channel_id=1, source_target_pairs={{0,4},{1,5},{4,8},{5,9},{8,12},{9,13},{12,14},{13,15},{14,10},{15,... | collective-permute-start | bytes 786440 | tf_op jit(solution)/shard_map/ppermute | solution.py:198
  93.3 4.3 %collective-permute-done.36.refs_2_ = bf16[64,2048]{1,0:T(8,128)(2,1)S(1)} collective-permute-done((bf16[64,2048]{1,0:T(8,128)(2,1)S(1)}, bf16[64,2048]{1,0:T(8,128)(2,1)S(1)}, u32[]{:S(2)}, u32[]{:S(2)}) %collective-permute-start.36) | collective-permute-done | bytes 262176 | tf_op jit(solution)/shard_map/ppermute | solution.py:198
  98.7 1.6 %collective-permute-start.35 = (bf16[64,2048]{1,0:T(8,128)(2,1)S(1)}, bf16[64,2048]{1,0:T(8,128)(2,1)S(1)}, u32[]{:S(2)}, u32[]{:S(2)}) collective-permute-start(bf16[64,2048]{1,0:T(8,128)(2,1)S(1)} %combine_rows.26), channel_id=1, source_target_pairs={{0,4},{1,5},{4,8},{5,9},{8,12},{9,13},{12,14},{13,15},{14,10},{15,... | collective-permute-start | bytes 786440 | tf_op jit(solution)/shard_map/ppermute | solution.py:198
  100.4 3.9 %collective-permute-done.31.refs_2_ = bf16[64,2048]{1,0:T(8,128)(2,1)S(1)} collective-permute-done((bf16[64,2048]{1,0:T(8,128)(2,1)S(1)}, bf16[64,2048]{1,0:T(8,128)(2,1)S(1)}, u32[]{:S(2)}, u32[]{:S(2)}) %collective-permute-start.31) | collective-permute-done | bytes 262176 | tf_op jit(solution)/shard_map/ppermute | solution.py:198
  104.4 1.6 %collective-permute-start.32 = (bf16[64,2048]{1,0:T(8,128)(2,1)S(1)}, bf16[64,2048]{1,0:T(8,128)(2,1)S(1)}, u32[]{:S(2)}, u32[]{:S(2)}) collective-permute-start(bf16[64,2048]{1,0:T(8,128)(2,1)S(1)} %combine_rows.23), channel_id=1, source_target_pairs={{0,4},{1,5},{4,8},{5,9},{8,12},{9,13},{12,14},{13,15},{14,10},{15,... | collective-permute-start | bytes 786440 | tf_op jit(solution)/shard_map/ppermute | solution.py:198
  106.6 2.2 %collective-permute-done.37.refs_7_ = bf16[64,2048]{1,0:T(8,128)(2,1)S(1)} collective-permute-done((bf16[64,2048]{1,0:T(8,128)(2,1)S(1)}, bf16[64,2048]{1,0:T(8,128)(2,1)S(1)}, u32[]{:S(2)}, u32[]{:S(2)}) %collective-permute-start.37) | collective-permute-done | bytes 262176 | tf_op jit(solution)/shard_map/ppermute | solution.py:198
  109.9 3.7 %collective-permute-done.32.refs_3_ = bf16[64,2048]{1,0:T(8,128)(2,1)S(1)} collective-permute-done((bf16[64,2048]{1,0:T(8,128)(2,1)S(1)}, bf16[64,2048]{1,0:T(8,128)(2,1)S(1)}, u32[]{:S(2)}, u32[]{:S(2)}) %collective-permute-start.32) | collective-permute-done | bytes 262176 | tf_op jit(solution)/shard_map/ppermute | solution.py:198
  (83 shorter events, 23.4 us)
Async XLA Ops:
  2.6 10.8 %collective-permute-start.1 = (bf16[64,2176]{1,0:T(8,128)(2,1)}, bf16[64,2176]{1,0:T(8,128)(2,1)S(1)}, u32[]{:S(2)}, u32[]{:S(2)}) collective-permute-start(bf16[64,2176]{1,0:T(8,128)(2,1)} %get-tuple-element.48), channel_id=1, source_target_pairs={{0,4},{1,5},{4,8},{5,9},{8,12},{9,13},{12,14},{13,15},{14,10},{15,... | collective-permute-start | bytes 835592 | tf_op jit(solution)/shard_map/ppermute | solution.py:198
  5.7 9.8 %collective-permute-start.2 = (bf16[64,2176]{1,0:T(8,128)(2,1)}, bf16[64,2176]{1,0:T(8,128)(2,1)S(1)}, u32[]{:S(2)}, u32[]{:S(2)}) collective-permute-start(bf16[64,2176]{1,0:T(8,128)(2,1)} %get-tuple-element.49), channel_id=1, source_target_pairs={{0,2},{1,3},{4,0},{5,1},{8,4},{9,5},{12,8},{13,9},{14,12},{15,13},... | collective-permute-start | bytes 835592 | tf_op jit(solution)/shard_map/ppermute | solution.py:198
  5.7 12.8 %collective-permute-start.7 = (bf16[64,2176]{1,0:T(8,128)(2,1)}, bf16[64,2176]{1,0:T(8,128)(2,1)S(1)}, u32[]{:S(2)}, u32[]{:S(2)}) collective-permute-start(bf16[64,2176]{1,0:T(8,128)(2,1)} %get-tuple-element.49), channel_id=1, source_target_pairs={{0,4},{1,5},{4,8},{5,9},{8,12},{9,13},{12,14},{13,15},{14,10},{15,... | collective-permute-start | bytes 835592 | tf_op jit(solution)/shard_map/ppermute | solution.py:198
  7.7 12.3 %collective-permute-start.8 = (bf16[64,2176]{1,0:T(8,128)(2,1)}, bf16[64,2176]{1,0:T(8,128)(2,1)S(1)}, u32[]{:S(2)}, u32[]{:S(2)}) collective-permute-start(bf16[64,2176]{1,0:T(8,128)(2,1)} %get-tuple-element.48), channel_id=1, source_target_pairs={{0,2},{1,3},{4,0},{5,1},{8,4},{9,5},{12,8},{13,9},{14,12},{15,13},... | collective-permute-start | bytes 835592 | tf_op jit(solution)/shard_map/ppermute | solution.py:198
  20.1 18.1 %collective-permute-start.9 = (bf16[256,2176]{1,0:T(8,128)(2,1)S(1)}, bf16[256,2176]{1,0:T(8,128)(2,1)S(1)}, u32[]{:S(2)}, u32[]{:S(2)}) collective-permute-start(bf16[256,2176]{1,0:T(8,128)(2,1)S(1)} %join_rows.4.refs_0_), channel_id=1, source_target_pairs={{0,1},{1,0},{2,3},{3,2},{4,5},{5,4},{6,7},{7,6},{8,9},{9,8},{10,11... | collective-permute-start | bytes 3342344 | tf_op jit(solution)/shard_map/ppermute | solution.py:203
  20.7 9.5 %collective-permute-start.3 = (bf16[64,2176]{1,0:T(8,128)(2,1)S(1)}, bf16[64,2176]{1,0:T(8,128)(2,1)S(1)}, u32[]{:S(2)}, u32[]{:S(2)}) collective-permute-start(bf16[64,2176]{1,0:T(8,128)(2,1)S(1)} %collective-permute-done.1.refs_0_), channel_id=1, source_target_pairs={{0,4},{1,5},{4,8},{5,9},{8,12},{9,13},{12,14},{13,15},{14,10},{15,... | collective-permute-start | bytes 835592 | tf_op jit(solution)/shard_map/ppermute | solution.py:198
  22.2 9.6 %collective-permute-start.4 = (bf16[64,2176]{1,0:T(8,128)(2,1)S(1)}, bf16[64,2176]{1,0:T(8,128)(2,1)S(1)}, u32[]{:S(2)}, u32[]{:S(2)}) collective-permute-start(bf16[64,2176]{1,0:T(8,128)(2,1)S(1)} %collective-permute-done.2.refs_3_), channel_id=1, source_target_pairs={{0,2},{1,3},{4,0},{5,1},{8,4},{9,5},{12,8},{13,9},{14,12},{15,13},... | collective-permute-start | bytes 835592 | tf_op jit(solution)/shard_map/ppermute | solution.py:198
  22.7 12.9 %collective-permute-start.12 = (bf16[64,2176]{1,0:T(8,128)(2,1)S(1)}, bf16[64,2176]{1,0:T(8,128)(2,1)S(1)}, u32[]{:S(2)}, u32[]{:S(2)}) collective-permute-start(bf16[64,2176]{1,0:T(8,128)(2,1)S(1)} %collective-permute-done.7.refs_1_), channel_id=1, source_target_pairs={{0,4},{1,5},{4,8},{5,9},{8,12},{9,13},{12,14},{13,15},{14,10},{15,... | collective-permute-start | bytes 835592 | tf_op jit(solution)/shard_map/ppermute | solution.py:198
  24.3 12.3 %collective-permute-start.13 = (bf16[64,2176]{1,0:T(8,128)(2,1)S(1)}, bf16[64,2176]{1,0:T(8,128)(2,1)S(1)}, u32[]{:S(2)}, u32[]{:S(2)}) collective-permute-start(bf16[64,2176]{1,0:T(8,128)(2,1)S(1)} %collective-permute-done.8.refs_2_), channel_id=1, source_target_pairs={{0,2},{1,3},{4,0},{5,1},{8,4},{9,5},{12,8},{13,9},{14,12},{15,13},... | collective-permute-start | bytes 835592 | tf_op jit(solution)/shard_map/ppermute | solution.py:198
  31.8 13.4 %collective-permute-start.10 = (bf16[128,2048]{1,0:T(8,128)(2,1)S(1)}, bf16[128,2048]{1,0:T(8,128)(2,1)S(1)}, u32[]{:S(2)}, u32[]{:S(2)}) collective-permute-start(bf16[128,2048]{1,0:T(8,128)(2,1)S(1)} %get-tuple-element.59), channel_id=1, source_target_pairs={{0,1},{1,0},{2,3},{3,2},{4,5},{5,4},{6,7},{7,6},{8,9},{9,8},{10,11... | collective-permute-start | bytes 1572872 | tf_op jit(solution)/shard_map/ppermute | solution.py:203
  31.8 13.2 %collective-permute-start.5 = (bf16[64,2176]{1,0:T(8,128)(2,1)S(1)}, bf16[64,2176]{1,0:T(8,128)(2,1)S(1)}, u32[]{:S(2)}, u32[]{:S(2)}) collective-permute-start(bf16[64,2176]{1,0:T(8,128)(2,1)S(1)} %collective-permute-done.3.refs_0_), channel_id=1, source_target_pairs={{0,4},{1,5},{4,8},{5,9},{8,12},{9,13},{12,14},{13,15},{14,10},{15,... | collective-permute-start | bytes 835592 | tf_op jit(solution)/shard_map/ppermute | solution.py:198
  35.6 9.6 %collective-permute-start.6 = (bf16[64,2176]{1,0:T(8,128)(2,1)S(1)}, bf16[64,2176]{1,0:T(8,128)(2,1)S(1)}, u32[]{:S(2)}, u32[]{:S(2)}) collective-permute-start(bf16[64,2176]{1,0:T(8,128)(2,1)S(1)} %collective-permute-done.4.refs_3_), channel_id=1, source_target_pairs={{0,2},{1,3},{4,0},{5,1},{8,4},{9,5},{12,8},{13,9},{14,12},{15,13},... | collective-permute-start | bytes 835592 | tf_op jit(solution)/shard_map/ppermute | solution.py:198
  36.6 10.6 %collective-permute-start.17 = (bf16[64,2176]{1,0:T(8,128)(2,1)S(1)}, bf16[64,2176]{1,0:T(8,128)(2,1)S(1)}, u32[]{:S(2)}, u32[]{:S(2)}) collective-permute-start(bf16[64,2176]{1,0:T(8,128)(2,1)S(1)} %collective-permute-done.12.refs_1_), channel_id=1, source_target_pairs={{0,4},{1,5},{4,8},{5,9},{8,12},{9,13},{12,14},{13,15},{14,10},{15,... | collective-permute-start | bytes 835592 | tf_op jit(solution)/shard_map/ppermute | solution.py:198
  38.2 10.9 %collective-permute-start.18 = (bf16[64,2176]{1,0:T(8,128)(2,1)S(1)}, bf16[64,2176]{1,0:T(8,128)(2,1)S(1)}, u32[]{:S(2)}, u32[]{:S(2)}) collective-permute-start(bf16[64,2176]{1,0:T(8,128)(2,1)S(1)} %collective-permute-done.13.refs_2_), channel_id=1, source_target_pairs={{0,2},{1,3},{4,0},{5,1},{8,4},{9,5},{12,8},{13,9},{14,12},{15,13},... | collective-permute-start | bytes 835592 | tf_op jit(solution)/shard_map/ppermute | solution.py:198
  49.2 9.1 %collective-permute-start.15 = (bf16[64,2176]{1,0:T(8,128)(2,1)S(1)}, bf16[64,2176]{1,0:T(8,128)(2,1)S(1)}, u32[]{:S(2)}, u32[]{:S(2)}) collective-permute-start(bf16[64,2176]{1,0:T(8,128)(2,1)S(1)} %collective-permute-done.5.refs_0_), channel_id=1, source_target_pairs={{0,4},{1,5},{4,8},{5,9},{8,12},{9,13},{12,14},{13,15},{14,10},{15,... | collective-permute-start | bytes 835592 | tf_op jit(solution)/shard_map/ppermute | solution.py:198
  50.8 8.7 %collective-permute-start.16 = (bf16[64,2176]{1,0:T(8,128)(2,1)S(1)}, bf16[64,2176]{1,0:T(8,128)(2,1)S(1)}, u32[]{:S(2)}, u32[]{:S(2)}) collective-permute-start(bf16[64,2176]{1,0:T(8,128)(2,1)S(1)} %collective-permute-done.6.refs_3_), channel_id=1, source_target_pairs={{0,2},{1,3},{4,0},{5,1},{8,4},{9,5},{12,8},{13,9},{14,12},{15,13},... | collective-permute-start | bytes 835592 | tf_op jit(solution)/shard_map/ppermute | solution.py:198
  59.8 10.5 %collective-permute-start.14 = (bf16[256,2176]{1,0:T(8,128)(2,1)S(1)}, bf16[256,2176]{1,0:T(8,128)(2,1)S(1)}, u32[]{:S(2)}, u32[]{:S(2)}) collective-permute-start(bf16[256,2176]{1,0:T(8,128)(2,1)S(1)} %join_rows.5.refs_0_), channel_id=1, source_target_pairs={{0,1},{1,0},{2,3},{3,2},{4,5},{5,4},{6,7},{7,6},{8,9},{9,8},{10,11... | collective-permute-start | bytes 3342344 | tf_op jit(solution)/shard_map/ppermute | solution.py:203
  65.8 10.9 %collective-permute-start.26 = (bf16[64,2048]{1,0:T(8,128)(2,1)S(1)}, bf16[64,2048]{1,0:T(8,128)(2,1)S(1)}, u32[]{:S(2)}, u32[]{:S(2)}) collective-permute-start(bf16[64,2048]{1,0:T(8,128)(2,1)S(1)} %combine_rows.18), channel_id=1, source_target_pairs={{0,2},{1,3},{4,0},{5,1},{8,4},{9,5},{12,8},{13,9},{14,12},{15,13},... | collective-permute-start | bytes 786440 | tf_op jit(solution)/shard_map/ppermute | solution.py:198
  66.4 10.3 %collective-permute-start.25 = (bf16[64,2048]{1,0:T(8,128)(2,1)S(1)}, bf16[64,2048]{1,0:T(8,128)(2,1)S(1)}, u32[]{:S(2)}, u32[]{:S(2)}) collective-permute-start(bf16[64,2048]{1,0:T(8,128)(2,1)S(1)} %combine_rows.17), channel_id=1, source_target_pairs={{0,4},{1,5},{4,8},{5,9},{8,12},{9,13},{12,14},{13,15},{14,10},{15,... | collective-permute-start | bytes 786440 | tf_op jit(solution)/shard_map/ppermute | solution.py:198
  68.1 12.3 %collective-permute-start.23 = (bf16[64,2048]{1,0:T(8,128)(2,1)S(1)}, bf16[64,2048]{1,0:T(8,128)(2,1)S(1)}, u32[]{:S(2)}, u32[]{:S(2)}) collective-permute-start(bf16[64,2048]{1,0:T(8,128)(2,1)S(1)} %combine_rows.16), channel_id=1, source_target_pairs={{0,4},{1,5},{4,8},{5,9},{8,12},{9,13},{12,14},{13,15},{14,10},{15,... | collective-permute-start | bytes 786440 | tf_op jit(solution)/shard_map/ppermute | solution.py:198
  69.8 10.6 %collective-permute-start.22 = (bf16[64,2048]{1,0:T(8,128)(2,1)S(1)}, bf16[64,2048]{1,0:T(8,128)(2,1)S(1)}, u32[]{:S(2)}, u32[]{:S(2)}) collective-permute-start(bf16[64,2048]{1,0:T(8,128)(2,1)S(1)} %combine_rows.15), channel_id=1, source_target_pairs={{0,2},{1,3},{4,0},{5,1},{8,4},{9,5},{12,8},{13,9},{14,12},{15,13},... | collective-permute-start | bytes 786440 | tf_op jit(solution)/shard_map/ppermute | solution.py:198
  80.4 12.9 %collective-permute-start.11 = (bf16[256,2048]{1,0:T(8,128)(2,1)S(1)}, bf16[256,2048]{1,0:T(8,128)(2,1)S(1)}, u32[]{:S(2)}, u32[]{:S(2)}) collective-permute-start(bf16[256,2048]{1,0:T(8,128)(2,1)S(1)} %get-tuple-element.62), channel_id=1, source_target_pairs={{0,1},{1,0},{2,3},{3,2},{4,5},{5,4},{6,7},{7,6},{8,9},{9,8},{10,11... | collective-permute-start | bytes 3145736 | tf_op jit(solution)/shard_map/ppermute | solution.py:203
  81.0 8.3 %collective-permute-start.33 = (bf16[64,2048]{1,0:T(8,128)(2,1)S(1)}, bf16[64,2048]{1,0:T(8,128)(2,1)S(1)}, u32[]{:S(2)}, u32[]{:S(2)}) collective-permute-start(bf16[64,2048]{1,0:T(8,128)(2,1)S(1)} %combine_rows.24), channel_id=1, source_target_pairs={{0,4},{1,5},{4,8},{5,9},{8,12},{9,13},{12,14},{13,15},{14,10},{15,... | collective-permute-start | bytes 786440 | tf_op jit(solution)/shard_map/ppermute | solution.py:198
  82.7 10.0 %collective-permute-start.28 = (bf16[64,2048]{1,0:T(8,128)(2,1)S(1)}, bf16[64,2048]{1,0:T(8,128)(2,1)S(1)}, u32[]{:S(2)}, u32[]{:S(2)}) collective-permute-start(bf16[64,2048]{1,0:T(8,128)(2,1)S(1)} %combine_rows.19), channel_id=1, source_target_pairs={{0,2},{1,3},{4,0},{5,1},{8,4},{9,5},{12,8},{13,9},{14,12},{15,13},... | collective-permute-start | bytes 786440 | tf_op jit(solution)/shard_map/ppermute | solution.py:198
  83.3 14.3 %collective-permute-start.36 = (bf16[64,2048]{1,0:T(8,128)(2,1)S(1)}, bf16[64,2048]{1,0:T(8,128)(2,1)S(1)}, u32[]{:S(2)}, u32[]{:S(2)}) collective-permute-start(bf16[64,2048]{1,0:T(8,128)(2,1)S(1)} %combine_rows.27), channel_id=1, source_target_pairs={{0,2},{1,3},{4,0},{5,1},{8,4},{9,5},{12,8},{13,9},{14,12},{15,13},... | collective-permute-start | bytes 786440 | tf_op jit(solution)/shard_map/ppermute | solution.py:198
  89.3 9.3 %collective-permute-start.34 = (bf16[64,2048]{1,0:T(8,128)(2,1)S(1)}, bf16[64,2048]{1,0:T(8,128)(2,1)S(1)}, u32[]{:S(2)}, u32[]{:S(2)}) collective-permute-start(bf16[64,2048]{1,0:T(8,128)(2,1)S(1)} %combine_rows.25), channel_id=1, source_target_pairs={{0,4},{1,5},{4,8},{5,9},{8,12},{9,13},{12,14},{13,15},{14,10},{15,... | collective-permute-start | bytes 786440 | tf_op jit(solution)/shard_map/ppermute | solution.py:198
  91.1 13.2 %collective-permute-start.31 = (bf16[64,2048]{1,0:T(8,128)(2,1)S(1)}, bf16[64,2048]{1,0:T(8,128)(2,1)S(1)}, u32[]{:S(2)}, u32[]{:S(2)}) collective-permute-start(bf16[64,2048]{1,0:T(8,128)(2,1)S(1)} %combine_rows.22), channel_id=1, source_target_pairs={{0,4},{1,5},{4,8},{5,9},{8,12},{9,13},{12,14},{13,15},{14,10},{15,... | collective-permute-start | bytes 786440 | tf_op jit(solution)/shard_map/ppermute | solution.py:198
  92.8 13.2 %collective-permute-start.29 = (bf16[64,2048]{1,0:T(8,128)(2,1)S(1)}, bf16[64,2048]{1,0:T(8,128)(2,1)S(1)}, u32[]{:S(2)}, u32[]{:S(2)}) collective-permute-start(bf16[64,2048]{1,0:T(8,128)(2,1)S(1)} %combine_rows.20), channel_id=1, source_target_pairs={{0,2},{1,3},{4,0},{5,1},{8,4},{9,5},{12,8},{13,9},{14,12},{15,13},... | collective-permute-start | bytes 786440 | tf_op jit(solution)/shard_map/ppermute | solution.py:198
  97.7 11.1 %collective-permute-start.37 = (bf16[64,2048]{1,0:T(8,128)(2,1)S(1)}, bf16[64,2048]{1,0:T(8,128)(2,1)S(1)}, u32[]{:S(2)}, u32[]{:S(2)}) collective-permute-start(bf16[64,2048]{1,0:T(8,128)(2,1)S(1)} %combine_rows.28), channel_id=1, source_target_pairs={{0,2},{1,3},{4,0},{5,1},{8,4},{9,5},{12,8},{13,9},{14,12},{15,13},... | collective-permute-start | bytes 786440 | tf_op jit(solution)/shard_map/ppermute | solution.py:198
  98.7 11.1 %collective-permute-start.35 = (bf16[64,2048]{1,0:T(8,128)(2,1)S(1)}, bf16[64,2048]{1,0:T(8,128)(2,1)S(1)}, u32[]{:S(2)}, u32[]{:S(2)}) collective-permute-start(bf16[64,2048]{1,0:T(8,128)(2,1)S(1)} %combine_rows.26), channel_id=1, source_target_pairs={{0,4},{1,5},{4,8},{5,9},{8,12},{9,13},{12,14},{13,15},{14,10},{15,... | collective-permute-start | bytes 786440 | tf_op jit(solution)/shard_map/ppermute | solution.py:198
  104.4 9.3 %collective-permute-start.32 = (bf16[64,2048]{1,0:T(8,128)(2,1)S(1)}, bf16[64,2048]{1,0:T(8,128)(2,1)S(1)}, u32[]{:S(2)}, u32[]{:S(2)}) collective-permute-start(bf16[64,2048]{1,0:T(8,128)(2,1)S(1)} %combine_rows.23), channel_id=1, source_target_pairs={{0,4},{1,5},{4,8},{5,9},{8,12},{9,13},{12,14},{13,15},{14,10},{15,... | collective-permute-start | bytes 786440 | tf_op jit(solution)/shard_map/ppermute | solution.py:198
  106.1 7.5 %collective-permute-start.30 = (bf16[64,2048]{1,0:T(8,128)(2,1)S(1)}, bf16[64,2048]{1,0:T(8,128)(2,1)S(1)}, u32[]{:S(2)}, u32[]{:S(2)}) collective-permute-start(bf16[64,2048]{1,0:T(8,128)(2,1)S(1)} %combine_rows.21), channel_id=1, source_target_pairs={{0,2},{1,3},{4,0},{5,1},{8,4},{9,5},{12,8},{13,9},{14,12},{15,13},... | collective-permute-start | bytes 786440 | tf_op jit(solution)/shard_map/ppermute | solution.py:198
  (12 other events, 54.7 us)
